TPU v7x, 128 devices: a whole 4x4x4 slice. The times are simulated.
128 devices in a mesh: row: 8 (over x, core), col: 16 (over z, y).
Axes of the slice: x: 4, y: 4, z: 4, core: 2. Of those that a mesh axis runs over, the one named last changes fastest.
Arguments:
- right_side: float32 [1024, 2, 256], P(('row', 'col')), may hold values from -12 to 12
- anchor: float32 [1024, 256], P(('row', 'col')), may hold values from 0.3 to 3
- tiles: float32 [1024, 4, 256, 256], P(('row', 'col')), may hold values from 0 to 1, as said below
- neighbours: int32 [1024, 4], P(('row', 'col')), may hold values from 0 to 1023, as said below
- owners: int32 [262144, 1], P(('row', 'col')), may hold values from 0 to 127; in each aligned block of 2048 rows (0 to 2047, 2048 to 4095, ...) at most 32 rows name the same one
- row_offset: int32 [262144], P(('row', 'col')), may hold values from 0 to 2047
- col_offset: int32 [262144], P(('row', 'col')), may hold values from 0 to 511
- macro_density: float32 [16384, 8192], P('row', 'col'), may hold values from 0.05 to 1
Outputs:
- solution: float32 [1024, 2, 256], P(('row', 'col'))
- density: float32 [16384, 8192], P('row', 'col')
Inputs may be any that keep to these rules, and one draw needn't show every extreme that they name: `owners`: at most 32 of the clusters of one device name the same owner; in every draw the clusters of some device name one owner exactly 32 times. `neighbours`: block b lies on device b // 8, and device d on mesh position (d // 16, d % 16) of row and col. Every tile names a block on the device of its own block row or on a device next to it along row, col or both (diagonals included). `tiles`: entries are positive.
All inputs are finite; a program needn't handle non-finite values.
Results may differ from a plain program's by a relative error of at most 0.0003.
Values sent between devices are 32-bit elements; how exact they have to be, the bound alone decides.
A program may use at most 128 MiB of HBM per device.

v0:
```python
import jax
import jax.numpy as jnp
from jax import lax
from jax.sharding import PartitionSpec as P

ITERS = 3
STEPS = 4


HIGH = lax.Precision.HIGHEST
RATE = 0.2


def passed_along(block, axis, distance):
    devices = range(lax.axis_size(axis))
    route = [(i - distance, i) for i in devices if i - distance in devices]
    return lax.ppermute(block, axis, route)


def extended(value, sides, width):
    for axis, dim in sides:
        size, length = (lax.axis_size(axis), value.shape[dim])
        up = [(i, (i + 1) % size) for i in range(size - 1)]
        down = [(j, i) for i, j in up]
        last = lax.slice_in_dim(value, length - width, length, axis=dim)
        leading = lax.slice_in_dim(value, 0, width, axis=dim)
        before = lax.ppermute(last, axis, up)
        after = lax.ppermute(leading, axis, down)
        value = jnp.concatenate([before, value, after], axis=dim)
    return value


def tile_terms(tiles, row_sums, col_sums, own_dir, remote):
    direct = jnp.einsum("bkij,bkcj->bci", tiles, remote, precision=HIGH)
    backward = jnp.einsum("bkij,bci->bkcj", tiles, own_dir, precision=HIGH)
    row_part = row_sums[:, None, :] * own_dir - direct
    col_part = col_sums[:, :, None, :] * remote - backward
    return (row_part, col_part)


def diffuse(padded):
    centre = padded[1:-1, 1:-1]
    return centre + RATE * (
        padded[2:, 1:-1] + padded[:-2, 1:-1] + padded[1:-1, 2:] + padded[1:-1, :-2] - 4.0 * centre
    )


def run_solver(image_of, curve_of, norm_of, start_rhs):
    solution = jnp.zeros_like(start_rhs)
    residual = start_rhs
    direction = start_rhs
    norm_now = norm_of(residual)
    for sweep in range(ITERS):
        image = image_of(direction)
        alpha = norm_now / curve_of(direction, image)
        solution = solution + alpha[None, :, None] * direction
        residual = residual - alpha[None, :, None] * image
        norm_next = norm_of(residual)
        direction = residual + (norm_next / norm_now)[None, :, None] * direction
        norm_now = norm_next
    return solution


def send_col(terms, offset):
    return passed_along(terms, "col", offset)


def send_row(terms, offset):
    return passed_along(terms, "row", offset)


def per_device(
    right_side, anchor, tiles, neighbours, owners, row_offset, col_offset, macro_density
):
    blocks_own = tiles.shape[0]
    fanout = tiles.shape[1]
    width_tile = tiles.shape[2]
    row_sums = jnp.sum(jnp.sum(tiles, axis=3), axis=1)
    col_sums = jnp.sum(tiles, axis=2)
    flat_nbr = neighbours.reshape(-1)
    rows_mesh = lax.axis_size("row")
    cols_mesh = lax.axis_size("col")
    devices_all = rows_mesh * cols_mesh
    device_me = lax.axis_index(("row", "col"))
    mesh_row = device_me // cols_mesh
    mesh_col = device_me % cols_mesh
    named_dev = flat_nbr // blocks_own
    near_slot = (
        (named_dev // cols_mesh - mesh_row + 1) * 3 + (named_dev % cols_mesh - mesh_col + 1)
    ) * blocks_own + flat_nbr % blocks_own
    slot_select = (near_slot[None, :] == lax.iota(jnp.int32, 9 * blocks_own)[:, None]).astype(
        jnp.float32
    )

    def image_of(direction):
        padded = extended(direction[None, None], (("row", 0), ("col", 1)), 1)
        near_blocks = padded.reshape(9 * blocks_own, 2, width_tile)
        remote = near_blocks[near_slot].reshape(blocks_own, fanout, 2, width_tile)
        row_part, col_part = tile_terms(tiles, row_sums, col_sums, direction, remote)
        flat_terms = col_part.reshape(blocks_own * fanout, 2 * width_tile)
        back = jnp.dot(slot_select, flat_terms, precision=HIGH).reshape(
            3, 3, blocks_own, 2, width_tile
        )
        merged_col = back[:, 1] + send_col(back[:, 0], -1) + send_col(back[:, 2], 1)
        incoming = merged_col[1] + send_row(merged_col[0], -1) + send_row(merged_col[2], 1)
        return anchor[:, None, :] * direction + row_part + incoming

    def curve_of(direction, image):
        return lax.psum(jnp.sum(direction * image, axis=(0, 2)), ("row", "col"))

    def norm_of(resid):
        return lax.psum(jnp.sum(resid * resid, axis=(0, 2)), ("row", "col"))

    solution = run_solver(image_of, curve_of, norm_of, right_side)
    clusters_own = blocks_own * width_tile
    by_coord = solution.transpose(1, 0, 2).reshape(2, clusters_own)
    pos_row = row_offset.astype(jnp.float32) + 3.0 * jnp.tanh(by_coord[0])
    pos_col = col_offset.astype(jnp.float32) + 3.0 * jnp.tanh(by_coord[1])
    capacity = max(2, 2 * clusters_own // devices_all)
    target = owners[:, 0]
    matches = (target[:, None] == lax.iota(jnp.int32, devices_all)[None, :]).astype(jnp.int32)
    before = jnp.cumsum(matches, axis=0) - matches
    rank_in = jnp.sum(before * matches, axis=1)
    slot_index = target * capacity + rank_in
    outgoing = jnp.full((2, devices_all * capacity), -1000.0, jnp.float32)
    outgoing = outgoing.at[:, slot_index].set(jnp.stack([pos_row, pos_col]))
    arrived = lax.all_to_all(
        outgoing.reshape(2, devices_all, capacity),
        ("row", "col"),
        split_axis=1,
        concat_axis=1,
        tiled=True,
    )
    arrived = arrived.reshape(2, devices_all * capacity)
    grid_rows = macro_density.shape[0]
    grid_cols = macro_density.shape[1]

    def window_of(position, limit):
        start_cell = jnp.clip(jnp.floor(position).astype(jnp.int32) - 7, 0, limit - 16)
        cells = lax.iota(jnp.int32, limit)[None, :]
        inside = ((cells >= start_cell[:, None]) & (cells < start_cell[:, None] + 16)).astype(
            jnp.float32
        )
        offset = cells.astype(jnp.float32) - position[:, None]
        return (jnp.exp(-0.5 * offset * offset) * inside).astype(jnp.bfloat16)

    bell_row = window_of(arrived[0], grid_rows)
    bell_col = window_of(arrived[1], grid_cols)
    spread = lax.dot_general(
        bell_row, bell_col, (((0,), (0,)), ((), ())), preferred_element_type=jnp.float32
    )
    field = macro_density + spread
    for sweep in range(STEPS):
        padded = extended(field, (("row", 0), ("col", 1)), 1)
        field = diffuse(padded)
    return (solution, field)


def solution(mesh):
    return jax.shard_map(
        per_device,
        mesh=mesh,
        in_specs=(
            P(("row", "col"), None, None),
            P(("row", "col"), None),
            P(("row", "col"), None, None, None),
            P(("row", "col"), None),
            P(("row", "col"), None),
            P(("row", "col")),
            P(("row", "col")),
            P("row", "col"),
        ),
        out_specs=(P(("row", "col"), None, None), P("row", "col")),
        check_vma=False,
    )
```

profile of v0, /device:TPU:34, one launch (start us, length us, event | category | flops | bytes accessed | tf_op | source)
XLA Modules:
  0.0 727.6 jit_solution(13097304338709061165)
XLA Ops:
  2.6 2.4 collective-permute-start
  6.0 4.1 fusion.113
  10.2 4.5 collective-permute-start.3
  16.6 6.5 collective-permute-done.2
  23.8 7.4 %fusion.48 = f32[8,4,2,256]{3,2,1,0:T(2,128)S(1)} fusion(f32[8,4,256,256]{3,2,1,0:T(8,128)} %param.10, f32[8,4,2,256]{3,2,1,0:T(2,128)S(1)} %bitcast.221, f32[8,4,256]{2,1,0:T(4,128)S(1)} %get-tuple-element.3, f32[8,2,256]{2,1,0:T(2,128)S(1)} %copy-done.4), kind=kOutput, calls=%fused_computation.71 | convolution fusion | flops 50364416 | bytes 8568832 | tf_op jit(solution)/shard_map/bkij,bci->bkcj/dot_general | solution.py:35
  33.6 6.0 collective-permute-start.4
  43.4 2.4 collective-permute-start.7
  45.8 2.6 collective-permute-done.7
  48.4 9.4 %multiply_reduce_fusion.3 = (f32[2]{0:T(128)S(1)}, f32[2]{0:T(128)S(1)}, f32[8,2,256]{2,1,0:T(2,128)S(1)}) fusion(f32[8,2,256]{2,1,0:T(2,128)S(1)} %copy-done.4, f32[8,2,256]{2,1,0:T(2,128)S(1)} %collective-permute-done.7, f32[8,2,256]{2,1,0:T(2,128)S(1)} %collective-permute-done.6, f32[3,8,2,256]{3,2,1,0:T(2,128)S(1)} %fusion.73, ...), kind=kOutput, calls=%fused_computation.168 | convolution fusion | flops 50376700 | bytes 8552464 | tf_op jit(solution)/shard_map/bkij,bkcj->bci/dot_general | solution.py:34
  57.8 65.5 %all-reduce = (f32[2]{0:T(128)S(1)}, f32[2]{0:T(128)S(1)}) all-reduce(f32[2]{0:T(128)S(1)} %get-tuple-element.7, f32[2]{0:T(128)S(1)} %get-tuple-element.6), channel_id=1, replica_groups=mesh['row'=8,'col'=16] {'row','col'}, use_global_device_ids=true, to_apply=%region_1.0 | all-reduce | flops 4 | bytes 32 | tf_op jit(solution)/shard_map/psum | solution.py:112
  123.5 62.4 %psum.44 = f32[2]{0:T(128)S(1)} all-reduce(f32[2]{0:T(128)S(1)} %get-tuple-element.12), channel_id=1, replica_groups=mesh['row'=8,'col'=16] {'row','col'}, use_global_device_ids=true, to_apply=%region_7.8 | all-reduce | flops 2 | bytes 16 | tf_op jit(solution)/shard_map/psum | solution.py:112
  186.0 3.5 collective-permute-start.9
  191.4 3.1 collective-permute-done.8
  194.6 4.2 collective-permute-start.11
  198.8 2.1 collective-permute-start.10
  200.9 6.0 collective-permute-done.10
  207.6 7.4 %fusion.47 = f32[8,4,2,256]{3,2,1,0:T(2,128)S(1)} fusion(f32[8,4,256,256]{3,2,1,0:T(8,128)} %param.10, f32[8,4,2,256]{3,2,1,0:T(2,128)S(1)} %bitcast.219, f32[8,4,256]{2,1,0:T(4,128)S(1)} %get-tuple-element.3, f32[8,2,256]{2,1,0:T(2,128)S(1)} %multiply_add_fusion.2), kind=kOutput, calls=%fused_computation.69 | convolution fusion | flops 50364416 | bytes 8568832 | tf_op jit(solution)/shard_map/bkij,bci->bkcj/dot_general | solution.py:35
  217.4 6.0 collective-permute-start.12
  227.1 2.4 collective-permute-start.15
  229.9 2.3 collective-permute-done.15
  232.2 9.3 %multiply_reduce_fusion.1 = (f32[2]{0:T(128)S(1)}, f32[8,2,256]{2,1,0:T(2,128)S(1)}) fusion(f32[8,2,256]{2,1,0:T(2,128)S(1)} %multiply_add_fusion.2, f32[8,2,256]{2,1,0:T(2,128)S(1)} %collective-permute-done.15, f32[8,2,256]{2,1,0:T(2,128)S(1)} %collective-permute-done.14, f32[3,8,2,256]{3,2,1,0:T(2,128)S(1)} %fusion.71, ...), kind=kOutput, calls=%fused_computation.164 | convolution fusion | flops 50368512 | bytes 8552456 | tf_op jit(solution)/shard_map/bkij,bkcj->bci/dot_general | solution.py:34
  241.5 63.6 %psum.45 = f32[2]{0:T(128)S(1)} all-reduce(f32[2]{0:T(128)S(1)} %get-tuple-element.52), channel_id=1, replica_groups=mesh['row'=8,'col'=16] {'row','col'}, use_global_device_ids=true, to_apply=%region_9.10 | all-reduce | flops 2 | bytes 16 | tf_op jit(solution)/shard_map/psum | solution.py:109
  305.3 62.1 %psum.46 = f32[2]{0:T(128)S(1)} all-reduce(f32[2]{0:T(128)S(1)} %get-tuple-element.10), channel_id=1, replica_groups=mesh['row'=8,'col'=16] {'row','col'}, use_global_device_ids=true, to_apply=%region_11.12 | all-reduce | flops 2 | bytes 16 | tf_op jit(solution)/shard_map/psum | solution.py:112
  367.5 3.8 collective-permute-start.17
  373.4 3.1 collective-permute-done.16
  376.5 4.5 collective-permute-start.19
  381.0 2.1 collective-permute-start.18
  383.6 5.5 collective-permute-done.18
  389.8 7.4 %fusion.46 = f32[8,4,2,256]{3,2,1,0:T(2,128)S(1)} fusion(f32[8,4,256,256]{3,2,1,0:T(8,128)} %param.10, f32[8,4,2,256]{3,2,1,0:T(2,128)S(1)} %bitcast.217, f32[8,4,256]{2,1,0:T(4,128)S(1)} %get-tuple-element.3, f32[8,2,256]{2,1,0:T(2,128)S(1)} %multiply_add_fusion.1), kind=kOutput, calls=%fused_computation.67 | convolution fusion | flops 50364416 | bytes 8568832 | tf_op jit(solution)/shard_map/bkij,bci->bkcj/dot_general | solution.py:35
  399.6 6.0 collective-permute-start.20
  409.3 2.4 collective-permute-start.23
  411.8 2.6 collective-permute-done.23
  414.4 9.3 %fusion.99 = f32[2]{0:T(128)S(1)} fusion(f32[8,2,256]{2,1,0:T(2,128)S(1)} %multiply_add_fusion.1, f32[8,2,256]{2,1,0:T(2,128)S(1)} %collective-permute-done.23, f32[8,2,256]{2,1,0:T(2,128)S(1)} %collective-permute-done.22, f32[3,8,2,256]{3,2,1,0:T(2,128)S(1)} %fusion.69, f32[8,4,2,256]{3,2,1,0:T(2,128)S(1)} %bitcast.218, f32[8,4,256,256]{3,2,1,0:T(8,128)} %param.10, ...), kind=kOutput, calls=%fused_computation.160 | convolution fusion | flops 50368512 | bytes 8536072 | tf_op jit(solution)/shard_map/bkij,bkcj->bci/dot_general | solution.py:34
  423.7 63.6 %psum.47 = f32[2]{0:T(128)S(1)} all-reduce(f32[2]{0:T(128)S(1)} %fusion.99), channel_id=1, replica_groups=mesh['row'=8,'col'=16] {'row','col'}, use_global_device_ids=true, to_apply=%region_13.14 | all-reduce | flops 2 | bytes 16 | tf_op jit(solution)/shard_map/psum | solution.py:109
  487.9 6.1 scatter_custom_fusion
  495.5 7.1 all-to-all-start
  502.6 8.0 %all-to-all-done = f32[2,128,32]{2,0,1:T(2,128)S(1)} async-done(((f32[2,128,32]{2,0,1:T(2,128)}), f32[2,128,32]{2,0,1:T(2,128)S(1)}, u32[]{:S(2)}, u32[]{:S(2)}) %all-to-all-start) | async-done | bytes 32800 | tf_op jit(solution)/shard_map/all_to_all | solution.py:127
  511.2 21.9 %fusion.41 = f32[2048,512]{1,0:T(8,128)S(1)} fusion(f32[2048,512]{1,0:T(8,128)} %param.15, f32[4096]{0:T(1024)S(1)} %squeeze.82, f32[512]{0:T(512)S(1)} %iota_convert_fusion.1, s32[4096]{0:T(1024)S(1)} %get-tuple-element.48, s32[4096]{0:T(1024)S(1)} %get-tuple-element.47, f32[4096]{0:T(1024)S(1)} %squeeze.81, f32[2048]{0:T(1024)S(1)} %iota_convert_fusion, ...), kind=kOutput, calls=%fused_computation.65 | convolution fusion | flops 8674869248 | bytes 8497152 | tf_op jit(solution)/shard_map/dot_general | solution.py:149
  535.1 2.5 collective-permute-start.24
  539.5 3.0 collective-permute-done.25
  542.5 13.5 %concatenate.90 = f32[2050,512]{1,0:T(8,128)} concatenate(f32[1,512]{1,0:T(1,128)S(1)} %collective-permute-done.25, f32[2048,512]{1,0:T(8,128)} %copy-done.3, f32[1,512]{1,0:T(1,128)S(1)} %collective-permute-done.24), dimensions={0} | concatenate | bytes 8396800 | tf_op jit(solution)/shard_map/concatenate | solution.py:29
  558.3 3.8 collective-permute-start.26
  562.4 2.1 collective-permute-start.27
  564.9 5.2 collective-permute-done.27
  570.5 12.7 %fusion.32 = f32[2048,512]{1,0:T(8,128)S(1)} fusion(f32[2048,512]{1,0:T(8,128)} %copy-done.3, f32[2050,512]{1,0:T(8,128)} %concatenate.90, f32[2050,1]{1,0:T(8,128)S(1)} %copy.61, f32[2050,1]{1,0:T(8,128)S(1)} %copy.59, f32[1,512]{1,0:T(1,128)S(1)} %collective-permute-done.25, f32[1,512]{1,0:T(1,128)S(1)} %collective-permute-done.24), kind=kLoop, calls=%fused_computation.53 | loop fusion | flops 11534336 | bytes 12607504 | tf_op jit(solution)/shard_map/add | solution.py:43
  587.2 2.4 collective-permute-start.29
  589.6 2.5 collective-permute-done.29
  592.1 13.5 %concatenate.95 = f32[2050,512]{1,0:T(8,128)} concatenate(f32[1,512]{1,0:T(1,128)S(1)} %collective-permute-done.29, f32[2048,512]{1,0:T(8,128)} %copy-done, f32[1,512]{1,0:T(1,128)S(1)} %collective-permute-done.28), dimensions={0} | concatenate | bytes 8396800 | tf_op jit(solution)/shard_map/concatenate | solution.py:29
  610.2 3.9 collective-permute-start.31
  614.5 3.3 collective-permute-done.31
  618.2 12.5 %fusion.26 = f32[2048,512]{1,0:T(8,128)S(1)} fusion(f32[2048,512]{1,0:T(8,128)} %copy-done, f32[2050,512]{1,0:T(8,128)} %concatenate.95, f32[2050,1]{1,0:T(8,128)S(1)} %copy.65, f32[2050,1]{1,0:T(8,128)S(1)} %copy.63, f32[1,512]{1,0:T(1,128)S(1)} %collective-permute-done.29, f32[1,512]{1,0:T(1,128)S(1)} %collective-permute-done.28), kind=kLoop, calls=%fused_computation.43 | loop fusion | flops 11534336 | bytes 12607504 | tf_op jit(solution)/shard_map/add | solution.py:43
  634.7 2.4 collective-permute-start.33
  637.1 2.5 collective-permute-done.33
  639.6 13.5 %concatenate.100 = f32[2050,512]{1,0:T(8,128)} concatenate(f32[1,512]{1,0:T(1,128)S(1)} %collective-permute-done.33, f32[2048,512]{1,0:T(8,128)} %copy-done.1, f32[1,512]{1,0:T(1,128)S(1)} %collective-permute-done.32), dimensions={0} | concatenate | bytes 8396800 | tf_op jit(solution)/shard_map/concatenate | solution.py:29
  657.7 3.9 collective-permute-start.35
  662.0 3.3 collective-permute-done.35
  665.7 12.5 %fusion.20 = f32[2048,512]{1,0:T(8,128)S(1)} fusion(f32[2048,512]{1,0:T(8,128)} %copy-done.1, f32[2050,512]{1,0:T(8,128)} %concatenate.100, f32[2050,1]{1,0:T(8,128)S(1)} %copy.69, f32[2050,1]{1,0:T(8,128)S(1)} %copy.67, f32[1,512]{1,0:T(1,128)S(1)} %collective-permute-done.33, f32[1,512]{1,0:T(1,128)S(1)} %collective-permute-done.32), kind=kLoop, calls=%fused_computation.33 | loop fusion | flops 11534336 | bytes 12607504 | tf_op jit(solution)/shard_map/add | solution.py:43
  682.2 2.4 collective-permute-start.37
  684.6 2.5 collective-permute-done.37
  687.1 13.5 %concatenate.105 = f32[2050,512]{1,0:T(8,128)} concatenate(f32[1,512]{1,0:T(1,128)S(1)} %collective-permute-done.37, f32[2048,512]{1,0:T(8,128)} %copy-done.2, f32[1,512]{1,0:T(1,128)S(1)} %collective-permute-done.36), dimensions={0} | concatenate | bytes 8396800 | tf_op jit(solution)/shard_map/concatenate | solution.py:29
  702.9 2.2 collective-permute-start.38
  705.4 3.9 collective-permute-start.39
  709.8 3.3 collective-permute-done.39
  713.5 13.7 %fusion.14 = f32[2048,512]{1,0:T(8,128)} fusion(f32[2048,512]{1,0:T(8,128)} %copy-done.2, f32[2050,512]{1,0:T(8,128)} %concatenate.105, f32[2050,1]{1,0:T(8,128)S(1)} %copy.73, f32[2050,1]{1,0:T(8,128)S(1)} %copy.71, f32[1,512]{1,0:T(1,128)S(1)} %collective-permute-done.37, f32[1,512]{1,0:T(1,128)S(1)} %collective-permute-done.36), kind=kLoop, calls=%fused_computation.23 | loop fusion | flops 11534336 | bytes 12607504 | tf_op jit(solution)/shard_map/add | solution.py:43
  (155 shorter events, 65.7 us)
Async XLA Ops:
  0.6 9.5 %collective-permute-start.1 = (f32[1,1,8,2,256]{4,3,2,1,0:T(2,128)}, f32[1,1,8,2,256]{4,3,2,1,0:T(2,128)S(1)}, u32[]{:S(2)}, u32[]{:S(2)}) collective-permute-start(f32[1,1,8,2,256]{4,3,2,1,0:T(2,128)} %bitcast.209), channel_id=1, source_target_pairs={{16,0},{32,16},{48,32},{64,48},{80,64},{96,80},{112,96},{17,1},{33... | collective-permute-start | bytes 49160 | tf_op jit(solution)/shard_map/ppermute | solution.py:28
  2.6 7.6 %collective-permute-start = (f32[1,1,8,2,256]{4,3,2,1,0:T(2,128)}, f32[1,1,8,2,256]{4,3,2,1,0:T(2,128)S(1)}, u32[]{:S(2)}, u32[]{:S(2)}) collective-permute-start(f32[1,1,8,2,256]{4,3,2,1,0:T(2,128)} %bitcast.210), channel_id=1, source_target_pairs={{0,16},{16,32},{32,48},{48,64},{64,80},{80,96},{96,112},{1,17},{17... | collective-permute-start | bytes 49160 | tf_op jit(solution)/shard_map/ppermute | solution.py:27
  6.0 4.2 copy-start.4
  10.2 6.4 collective-permute-start.3
  14.6 8.5 %collective-permute-start.2 = (f32[3,1,8,2,256]{4,3,2,1,0:T(2,128)S(1)}, f32[3,1,8,2,256]{4,3,2,1,0:T(2,128)S(1)}, u32[]{:S(2)}, u32[]{:S(2)}) collective-permute-start(f32[3,1,8,2,256]{4,3,2,1,0:T(2,128)S(1)} %pad_maximum_fusion.19), channel_id=1, source_target_pairs={{0,1},{1,2},{2,3},{3,4},{4,5},{5,6},{6,7},{7,8},{8,9},{9,10},{10,1... | collective-permute-start | bytes 147464 | tf_op jit(solution)/shard_map/ppermute | solution.py:27
  23.8 24.6 %copy-start.6 = (f32[8,256]{1,0:T(8,128)S(1)}, f32[8,256]{1,0:T(8,128)}, u32[]{:S(2)}) copy-start(f32[8,256]{1,0:T(8,128)} %param.9) | copy-start | bytes 24580
  31.7 8.1 %collective-permute-start.5 = (f32[3,8,2,256]{3,2,1,0:T(2,128)S(1)}, f32[3,8,2,256]{3,2,1,0:T(2,128)S(1)}, u32[]{:S(2)}, u32[]{:S(2)}) collective-permute-start(f32[3,8,2,256]{3,2,1,0:T(2,128)S(1)} %bitcast.247), channel_id=1, source_target_pairs={{0,1},{1,2},{2,3},{3,4},{4,5},{5,6},{6,7},{7,8},{8,9},{9,10},{10,1... | collective-permute-start | bytes 147464 | tf_op jit(solution)/shard_map/ppermute | solution.py:17
  33.6 7.8 %collective-permute-start.4 = (f32[3,8,2,256]{3,2,1,0:T(2,128)S(1)}, f32[3,8,2,256]{3,2,1,0:T(2,128)S(1)}, u32[]{:S(2)}, u32[]{:S(2)}) collective-permute-start(f32[3,8,2,256]{3,2,1,0:T(2,128)S(1)} %bitcast.244), channel_id=1, source_target_pairs={{1,0},{2,1},{3,2},{4,3},{5,4},{6,5},{7,6},{8,7},{9,8},{10,9},{11,1... | collective-permute-start | bytes 147464 | tf_op jit(solution)/shard_map/ppermute | solution.py:17
  41.4 4.3 collective-permute-start.6
  43.4 5.1 collective-permute-start.7
  186.0 5.4 collective-permute-start.9
  189.5 5.1 collective-permute-start.8
  194.6 6.3 collective-permute-start.11
  198.8 8.1 %collective-permute-start.10 = (f32[3,1,8,2,256]{4,3,2,1,0:T(2,128)S(1)}, f32[3,1,8,2,256]{4,3,2,1,0:T(2,128)S(1)}, u32[]{:S(2)}, u32[]{:S(2)}) collective-permute-start(f32[3,1,8,2,256]{4,3,2,1,0:T(2,128)S(1)} %pad_maximum_fusion.20), channel_id=1, source_target_pairs={{0,1},{1,2},{2,3},{3,4},{4,5},{5,6},{6,7},{7,8},{8,9},{9,10},{10,1... | collective-permute-start | bytes 147464 | tf_op jit(solution)/shard_map/ppermute | solution.py:27
  207.6 15.8 %copy-start.5 = (s32[2048,1]{0,1:T(1,128)S(1)}, s32[2048,1]{0,1:T(1,128)}, u32[]{:S(2)}) copy-start(s32[2048,1]{0,1:T(1,128)} %param.12) | copy-start | bytes 24580
  215.4 8.1 %collective-permute-start.13 = (f32[3,8,2,256]{3,2,1,0:T(2,128)S(1)}, f32[3,8,2,256]{3,2,1,0:T(2,128)S(1)}, u32[]{:S(2)}, u32[]{:S(2)}) collective-permute-start(f32[3,8,2,256]{3,2,1,0:T(2,128)S(1)} %bitcast.246), channel_id=1, source_target_pairs={{0,1},{1,2},{2,3},{3,4},{4,5},{5,6},{6,7},{7,8},{8,9},{9,10},{10,1... | collective-permute-start | bytes 147464 | tf_op jit(solution)/shard_map/ppermute | solution.py:17
  217.4 7.8 %collective-permute-start.12 = (f32[3,8,2,256]{3,2,1,0:T(2,128)S(1)}, f32[3,8,2,256]{3,2,1,0:T(2,128)S(1)}, u32[]{:S(2)}, u32[]{:S(2)}) collective-permute-start(f32[3,8,2,256]{3,2,1,0:T(2,128)S(1)} %bitcast.243), channel_id=1, source_target_pairs={{1,0},{2,1},{3,2},{4,3},{5,4},{6,5},{7,6},{8,7},{9,8},{10,9},{11,1... | collective-permute-start | bytes 147464 | tf_op jit(solution)/shard_map/ppermute | solution.py:17
  225.2 4.7 collective-permute-start.14
  227.1 5.1 collective-permute-start.15
  367.5 5.8 collective-permute-start.17
  371.4 5.1 collective-permute-start.16
  376.5 7.1 collective-permute-start.19
  381.0 8.1 %collective-permute-start.18 = (f32[3,1,8,2,256]{4,3,2,1,0:T(2,128)S(1)}, f32[3,1,8,2,256]{4,3,2,1,0:T(2,128)S(1)}, u32[]{:S(2)}, u32[]{:S(2)}) collective-permute-start(f32[3,1,8,2,256]{4,3,2,1,0:T(2,128)S(1)} %pad_maximum_fusion.21), channel_id=1, source_target_pairs={{0,1},{1,2},{2,3},{3,4},{4,5},{5,6},{6,7},{7,8},{8,9},{9,10},{10,1... | collective-permute-start | bytes 147464 | tf_op jit(solution)/shard_map/ppermute | solution.py:27
  397.7 8.6 %collective-permute-start.21 = (f32[3,8,2,256]{3,2,1,0:T(2,128)S(1)}, f32[3,8,2,256]{3,2,1,0:T(2,128)S(1)}, u32[]{:S(2)}, u32[]{:S(2)}) collective-permute-start(f32[3,8,2,256]{3,2,1,0:T(2,128)S(1)} %bitcast.245), channel_id=1, source_target_pairs={{0,1},{1,2},{2,3},{3,4},{4,5},{5,6},{6,7},{7,8},{8,9},{9,10},{10,1... | collective-permute-start | bytes 147464 | tf_op jit(solution)/shard_map/ppermute | solution.py:17
  399.6 7.8 %collective-permute-start.20 = (f32[3,8,2,256]{3,2,1,0:T(2,128)S(1)}, f32[3,8,2,256]{3,2,1,0:T(2,128)S(1)}, u32[]{:S(2)}, u32[]{:S(2)}) collective-permute-start(f32[3,8,2,256]{3,2,1,0:T(2,128)S(1)} %bitcast.242), channel_id=1, source_target_pairs={{1,0},{2,1},{3,2},{4,3},{5,4},{6,5},{7,6},{8,7},{9,8},{10,9},{11,1... | collective-permute-start | bytes 147464 | tf_op jit(solution)/shard_map/ppermute | solution.py:17
  407.4 4.4 collective-permute-start.22
  409.3 5.1 collective-permute-start.23
  411.8 75.7 %copy-start.8 = (s32[2048]{0:T(1024)S(1)}, s32[2048]{0:T(1024)}, u32[]{:S(2)}) copy-start(s32[2048]{0:T(1024)} %param.13) | copy-start | bytes 24580
  411.8 75.7 %copy-start.9 = (s32[2048]{0:T(1024)S(1)}, s32[2048]{0:T(1024)}, u32[]{:S(2)}) copy-start(s32[2048]{0:T(1024)} %param.14) | copy-start | bytes 24580
  487.4 45.7 %copy-start.7 = (f32[8,2,256]{2,1,0:T(2,128)}, f32[8,2,256]{2,1,0:T(2,128)S(1)}, u32[]{:S(2)}) copy-start(f32[8,2,256]{2,1,0:T(2,128)S(1)} %multiply_add_fusion) | copy-start | bytes 49156
  495.5 15.1 %all-to-all-start = ((f32[2,128,32]{2,0,1:T(2,128)}), f32[2,128,32]{2,0,1:T(2,128)S(1)}, u32[]{:S(2)}, u32[]{:S(2)}) async-start(f32[2,128,32]{2,0,1:T(2,128)} %copy.57), calls=%async_computation | async-start | bytes 262144 | tf_op jit(solution)/shard_map/all_to_all | solution.py:127
  533.1 2.0 copy-start.3
  535.1 4.4 collective-permute-start.24
  537.6 4.9 collective-permute-start.25
  558.3 6.2 collective-permute-start.26
  562.4 7.7 %collective-permute-start.27 = (f32[2050,1]{0,1:T(1,128)S(1)}, f32[2050,1]{0,1:T(1,128)S(1)}, u32[]{:S(2)}, u32[]{:S(2)}) collective-permute-start(f32[2050,1]{0,1:T(1,128)S(1)} %copy.60), channel_id=1, source_target_pairs={{0,1},{1,2},{2,3},{3,4},{4,5},{5,6},{6,7},{7,8},{8,9},{9,10},{10,1... | collective-permute-start | bytes 24608 | tf_op jit(solution)/shard_map/ppermute | solution.py:27
  583.2 2.0 copy-start
  585.3 4.3 collective-permute-start.28
  587.2 4.9 collective-permute-start.29
  607.9 6.2 collective-permute-start.30
  610.2 7.7 %collective-permute-start.31 = (f32[2050,1]{0,1:T(1,128)S(1)}, f32[2050,1]{0,1:T(1,128)S(1)}, u32[]{:S(2)}, u32[]{:S(2)}) collective-permute-start(f32[2050,1]{0,1:T(1,128)S(1)} %copy.64), channel_id=1, source_target_pairs={{0,1},{1,2},{2,3},{3,4},{4,5},{5,6},{6,7},{7,8},{8,9},{9,10},{10,1... | collective-permute-start | bytes 24608 | tf_op jit(solution)/shard_map/ppermute | solution.py:27
  630.8 2.0 copy-start.1
  632.8 4.3 collective-permute-start.32
  634.7 4.9 collective-permute-start.33
  655.4 6.2 collective-permute-start.34
  657.7 7.7 %collective-permute-start.35 = (f32[2050,1]{0,1:T(1,128)S(1)}, f32[2050,1]{0,1:T(1,128)S(1)}, u32[]{:S(2)}, u32[]{:S(2)}) collective-permute-start(f32[2050,1]{0,1:T(1,128)S(1)} %copy.68), channel_id=1, source_target_pairs={{0,1},{1,2},{2,3},{3,4},{4,5},{5,6},{6,7},{7,8},{8,9},{9,10},{10,1... | collective-permute-start | bytes 24608 | tf_op jit(solution)/shard_map/ppermute | solution.py:27
  678.3 2.0 copy-start.2
  680.3 4.3 collective-permute-start.36
  682.2 4.9 collective-permute-start.37
  702.9 6.5 collective-permute-start.38
  705.4 7.7 %collective-permute-start.39 = (f32[2050,1]{0,1:T(1,128)S(1)}, f32[2050,1]{0,1:T(1,128)S(1)}, u32[]{:S(2)}, u32[]{:S(2)}) collective-permute-start(f32[2050,1]{0,1:T(1,128)S(1)} %copy.72), channel_id=1, source_target_pairs={{0,1},{1,2},{2,3},{3,4},{4,5},{5,6},{6,7},{7,8},{8,9},{9,10},{10,1... | collective-permute-start | bytes 24608 | tf_op jit(solution)/shard_map/ppermute | solution.py:27
where the time goes:
time: 739 us; the launch traced here: 728 us
  blocking collectives  317 us (43%)
  starting transfers between devices  120 us (16%)
  local copies, waits for them, and re-layouts  87.6 us (12%)
  matrix products  73 us (10%)
  waiting for transfers between devices  69.9 us (9%)
  other arithmetic  58 us (8%)
    psum x3, blocking collectives, norm_of(): return lax.psum(jnp.sum(resid * resid, axis=(0, 2)), ('row', 'col'))  190 us
    psum x2, blocking collectives, curve_of(): return lax.psum(jnp.sum(direction * image, axis=(0, 2)), ('row', 'col'))  127 us
    concatenate x4, local copies, waits for them, and re-layouts, extended(): value = jnp.concatenate([before, value, after], axis=dim)  54.2 us
    add x4, other arithmetic, diffuse(): centre + RATE * (padded[2:, 1:-1] + padded[:-2, 1:-1] + padded[1:-1, 2:]...  51.5 us
    ppermute x14, waiting for transfers between devices, extended(): before = lax.ppermute(last, axis, up)  49.9 us
    ppermute x14, starting transfers between devices, extended(): after = lax.ppermute(leading, axis, down)  40.5 us
    ppermute x12, starting transfers between devices, passed_along(): return lax.ppermute(block, axis, route)  36.8 us
    ppermute x14, starting transfers between devices, extended(): before = lax.ppermute(last, axis, up)  35.4 us
  transfers between devices with their start and end apart: 41, of which 21 were waited for; matrix products, arithmetic and copies ran while one was open for 1% of the time, Pallas kernels for 0%

commit v1 on v0

v1 whole, which is shorter than its diff:
```python
import functools

import jax
import jax.numpy as jnp
from jax import lax
from jax.experimental import pallas as pl
from jax.experimental.pallas import tpu as pltpu
from jax.sharding import PartitionSpec as P

MESH = pl.DeviceIdType.MESH
F32 = jnp.float32
BF16 = jnp.bfloat16
STEPS = 4
CAP = 32
NONE = -1000.0
AROUND = [(dr, dc) for dr in (-1, 0, 1) for dc in (-1, 0, 1)]


def nt_dot(a, b):
    return lax.dot_general(a, b, (((1,), (1,)), ((), ())), preferred_element_type=F32)


def nn_dot(a, b):
    return jnp.dot(a, b, preferred_element_type=F32)


def split3(x):
    hi = x.astype(BF16)
    rest = x - hi.astype(F32)
    mid = rest.astype(BF16)
    low = (rest - mid.astype(F32)).astype(BF16)
    return hi, mid, low


def iota(shape, dim):
    return lax.broadcasted_iota(jnp.int32, shape, dim)


def remote(src, dst, send, recv, row, col):
    return pltpu.make_async_remote_copy(
        src_ref=src, dst_ref=dst, send_sem=send, recv_sem=recv,
        device_id={"row": row, "col": col}, device_id_type=MESH,
    )


def solve_kernel(
    n_row, n_col,
    nbr_ref, rhs_ref, anchor_ref, owner_ref, roff_ref, coff_ref, tiles_ref,
    sol_ref, arrived_ref,
    stage, thi, tlo, xbuf, sel, spread_sel, gath, terms, back, recv,
    ar_row, ar_col, own_hot, rank_sc, out_rows, mid_rows,
    tile_sem, fs, fr, bs, br, rs, rr, cs, cr, away1, got, away2, land, keep_sem,
):
    n_blk, fan, side, _ = thi.shape
    rows = 2 * n_blk
    q_own = n_blk * fan * 8
    q_all = q_own + n_blk * 8
    n_dev = n_row * n_col
    me_r = lax.axis_index("row")
    me_c = lax.axis_index("col")

    for b in range(n_blk):
        pltpu.make_async_copy(tiles_ref.at[b], stage.at[b], tile_sem.at[b]).start()

    barrier = pltpu.get_barrier_semaphore()
    peers = [(d, 0) for d in range(1, n_row)] + [(0, d) for d in range(1, n_col)]
    peers += [(dr, dc) for dr, dc in AROUND if dr and dc]
    for dr, dc in peers:
        pl.semaphore_signal(
            barrier, inc=1,
            device_id={"row": lax.rem(me_r + dr + n_row, n_row), "col": lax.rem(me_c + dc + n_col, n_col)},
            device_id_type=MESH,
        )

    own_lo = 4 * rows
    below = iota((side - 9 * rows, side), 0)
    for it in range(3):
        xbuf[it, 9 * rows:side, :] = jnp.where(below == 0, 1.0, 0.0)
    for b in range(n_blk):
        xbuf[0, own_lo + 2 * b:own_lo + 2 * b + 2, :] = rhs_ref[b]

    pl.semaphore_wait(barrier, len(peers))

    def x_rows(it, g):
        return xbuf.at[it, pl.ds(g * rows, rows)]

    pending = []

    def forward(it):
        for g, (dr, dc) in enumerate(AROUND):
            if g == 4:
                continue
            copy = remote(
                x_rows(it, 4), x_rows(it, 8 - g), fs.at[it, g], fr.at[it, 8 - g],
                lax.rem(me_r + dr + n_row, n_row), lax.rem(me_c + dc + n_col, n_col),
            )
            copy.start()
            pending.append(copy)

    def forward_wait(it):
        for g in range(9):
            if g != 4:
                remote(x_rows(it, 4), x_rows(it, g), fs.at[it, g], fr.at[it, g], me_r, me_c).wait_recv()

    def backward(it):
        for g, (dr, dc) in enumerate(AROUND):
            if g == 4:
                continue
            copy = remote(
                back.at[it, pl.ds(g * rows, rows)], recv.at[it, 8 - g], bs.at[it, g], br.at[it, 8 - g],
                lax.rem(me_r + dr + n_row, n_row), lax.rem(me_c + dc + n_col, n_col),
            )
            copy.start()
            pending.append(copy)

    def backward_wait(it):
        for g in range(9):
            if g != 4:
                remote(back.at[it, pl.ds(g * rows, rows)], recv.at[it, g], bs.at[it, g], br.at[it, g], me_r, me_c).wait_recv()

    forward(0)

    ones_row = 9 * rows
    lane3 = iota((8, 3 * side), 1)
    part_row = iota((8, 1), 0)
    base_col = jnp.where(
        part_row < 6, (part_row // 2) * side + lax.rem(part_row, 2), jnp.where(part_row == 6, ones_row, -1)
    )
    moves = (part_row < 6).astype(jnp.int32)

    def select_row(q, slot):
        sel[q:q + 8, :] = (lane3 == base_col + moves * (2 * slot)).astype(F32).astype(BF16)

    for b in range(n_blk):
        for k in range(fan):
            named = nbr_ref[b, k]
            dev = named // n_blk
            slot = ((dev // n_col - me_r + 1) * 3 + (lax.rem(dev, n_col) - me_c + 1)) * n_blk + lax.rem(named, n_blk)
            select_row((b * fan + k) * 8, slot)
        select_row(q_own + b * 8, 4 * n_blk + b)
    sel_t = sel[:, 0:side].astype(F32) + sel[:, side:2 * side].astype(F32) + sel[:, 2 * side:].astype(F32)
    spread_sel[...] = jnp.transpose(jnp.concatenate([sel_t, jnp.zeros((384 - q_all, side), F32)], axis=0)).astype(BF16)
    terms[...] = jnp.zeros_like(terms)

    upper = (iota((side, side), 0) < iota((side, side), 1)).astype(F32).astype(BF16)

    count = jnp.zeros((n_dev, 1), F32)
    for b in range(n_blk):
        hot = (owner_ref[b:b + 1, :] == iota((n_dev, side), 0)).astype(F32)
        own_hot[b] = hot.astype(BF16)
        before = nn_dot(hot.astype(BF16), upper) + count
        rank_sc[b:b + 1, :] = jnp.sum(hot * before, axis=0, keepdims=True)
        count = count + jnp.sum(hot, axis=1, keepdims=True)

    def split_block(b, carry):
        pltpu.make_async_copy(tiles_ref.at[b], stage.at[b], tile_sem.at[b]).wait()
        for k in range(fan):
            t = stage[b, k]
            hi = t.astype(BF16)
            thi[b, k] = hi
            tlo[b, k] = (t - hi.astype(F32)).astype(BF16)
        return carry

    lax.fori_loop(0, n_blk, split_block, 0)

    def apply(it, after_forward=None):
        forward_wait(it)
        if after_forward is not None:
            after_forward()
        parts = jnp.concatenate(split3(xbuf[it]), axis=0)
        gath[...] = nn_dot(sel[...], parts)

        def one_block(b, carry):
            own = gath[pl.ds(pl.multiple_of(q_own + b * 8, 8), 8), :]
            own_b = own.astype(BF16)
            total = jnp.zeros((8, side), F32)
            for k in range(fan):
                q = pl.multiple_of((b * fan + k) * 8, 8)
                far = gath[pl.ds(q, 8), :]
                far_b = far.astype(BF16)
                total = total + nt_dot(far_b, thi[b, k]) + nt_dot(far_b, tlo[b, k])
                down = nn_dot(own_b, thi[b, k]) + nn_dot(own_b, tlo[b, k])
                terms[pl.ds(q, 8), :] = down[6:7, :] * far - down
            weight = total[6:7, :] + anchor_ref[pl.ds(b, 1), :]
            terms[pl.ds(pl.multiple_of(q_own + b * 8, 8), 8), :] = weight * own - total
            return carry

        lax.fori_loop(0, n_blk, one_block, 0)
        hi, mid, low = split3(terms[...])
        where_to = spread_sel[0:9 * rows, :]
        back[it] = nn_dot(where_to, hi) + nn_dot(where_to, mid) + nn_dot(where_to, low)
        backward(it)

    def applied(it):
        backward_wait(it)
        image = back[it, own_lo:own_lo + rows, :]
        for g in range(9):
            if g != 4:
                image = image + recv[it, g]
        return image

    def dots_start(it, pairs):
        lane = iota((8, 128), 1)
        tile = jnp.zeros((8, 128), F32)
        for d, (a, b) in enumerate(pairs):
            e = a * b
            e = e[0:8] + e[8:16]
            tile = jnp.where(lane == d, jnp.sum(e, axis=1, keepdims=True), tile)
        ar_row[it, me_r] = tile
        for d in range(1, n_row):
            copy = remote(
                ar_row.at[it, me_r], ar_row.at[it, me_r], rs.at[it, d], rr.at[it, me_r],
                lax.rem(me_r + d, n_row), me_c,
            )
            copy.start()
            pending.append(copy)

    def dots_middle(it):
        for d in range(1, n_row):
            far = lax.rem(me_r + d, n_row)
            remote(ar_row.at[it, far], ar_row.at[it, far], rs.at[it, d], rr.at[it, far], me_r, me_c).wait_recv()
        ar_col[it, me_c] = jnp.sum(ar_row[it], axis=0)
        for d in range(1, n_col):
            copy = remote(
                ar_col.at[it, me_c], ar_col.at[it, me_c], cs.at[it, d], cr.at[it, me_c],
                me_r, lax.rem(me_c + d, n_col),
            )
            copy.start()
            pending.append(copy)

    def dots_end(it, n):
        for d in range(1, n_col):
            far = lax.rem(me_c + d, n_col)
            remote(ar_col.at[it, far], ar_col.at[it, far], cs.at[it, d], cr.at[it, far], me_r, me_c).wait_recv()
        t = jnp.sum(ar_col[it], axis=0)
        t = t + pltpu.roll(t, 4, 0)
        t = t + pltpu.roll(t, 2, 0)
        return [t[:, d:d + 1] for d in range(n)]

    def times(c, v):
        return jnp.concatenate([c] * (rows // 8), axis=0) * v

    r0 = xbuf[0, own_lo:own_lo + rows, :]
    apply(0)
    w0 = applied(0)
    xbuf[1, own_lo:own_lo + rows, :] = w0
    forward(1)
    dots_start(0, [(r0, r0), (r0, w0)])
    apply(1, lambda: dots_middle(0))
    gamma0, curve0 = dots_end(0, 2)
    alpha0 = gamma0 / curve0
    z0 = applied(1)
    w1 = w0 - times(alpha0, z0)
    xbuf[2, own_lo:own_lo + rows, :] = w1
    forward(2)
    r1 = r0 - times(alpha0, w0)
    dots_start(1, [(r1, r1), (r1, w1), (r1, w0)])
    apply(2, lambda: dots_middle(1))
    gamma1, r1w1, r1w0 = dots_end(1, 3)
    beta0 = gamma1 / gamma0
    curve1 = r1w1 + 2.0 * beta0 * r1w0 + beta0 * beta0 * curve0
    alpha1 = gamma1 / curve1
    p1 = r1 + times(beta0, r0)
    s1 = w1 + times(beta0, w0)
    z1 = applied(2)
    q1 = z1 + times(beta0, z0)
    r2 = r1 - times(alpha1, s1)
    w2 = w1 - times(alpha1, q1)
    dots_start(2, [(r2, r2), (r2, w2), (r2, s1)])
    dots_middle(2)
    gamma2, r2w2, r2s1 = dots_end(2, 3)
    beta1 = gamma2 / gamma1
    curve2 = r2w2 + 2.0 * beta1 * r2s1 + beta1 * beta1 * curve1
    alpha2 = gamma2 / curve2
    x = times(alpha0, r0) + times(alpha1, p1) + times(alpha2, r2 + times(beta1, p1))
    for b in range(n_blk):
        sol_ref[b] = x[2 * b:2 * b + 2, :]

    moved = 3.0 * jnp.tanh(x)
    table = jnp.zeros((n_dev, 128), F32)
    lane_rank = iota((2 * CAP, side), 0)
    for b in range(n_blk):
        pos_row = roff_ref[b:b + 1, :].astype(F32) + moved[2 * b:2 * b + 1, :]
        pos_col = coff_ref[b:b + 1, :].astype(F32) + moved[2 * b + 1:2 * b + 2, :]
        rank = rank_sc[b:b + 1, :].astype(jnp.int32)
        placed = jnp.where(lane_rank == rank, pos_row, jnp.where(lane_rank == rank + CAP, pos_col, 0.0))
        placed = jnp.concatenate([placed, jnp.zeros((128 - 2 * CAP, side), F32)], axis=0)
        for part in split3(placed):
            table = table + nt_dot(own_hot[b], part)
    lane_of = lax.rem(iota((n_dev, 128), 1), CAP).astype(F32)
    table = jnp.where(lane_of < count, table, NONE)
    for o in range(n_dev):
        out_rows[o // n_col, o % n_col] = table[o:o + 1, :]

    keep = pltpu.make_async_copy(out_rows.at[me_r], mid_rows.at[:, me_r], keep_sem.at[0])
    keep.start()
    for d in range(1, n_row):
        far = lax.rem(me_r + d, n_row)
        copy = remote(out_rows.at[far], mid_rows.at[:, me_r], away1.at[d], got.at[me_r], far, me_c)
        copy.start()
        pending.append(copy)
    keep.wait()
    for d in range(1, n_row):
        far = lax.rem(me_r + d, n_row)
        remote(out_rows.at[far], mid_rows.at[:, far], away1.at[d], got.at[far], me_r, me_c).wait_recv()
    keep2 = pltpu.make_async_copy(mid_rows.at[me_c], arrived_ref.at[me_c], keep_sem.at[1])
    keep2.start()
    for d in range(1, n_col):
        far = lax.rem(me_c + d, n_col)
        copy = remote(mid_rows.at[far], arrived_ref.at[me_c], away2.at[d], land.at[me_c], me_r, far)
        copy.start()
        pending.append(copy)
    keep2.wait()
    for d in range(1, n_col):
        far = lax.rem(me_c + d, n_col)
        remote(mid_rows.at[far], arrived_ref.at[far], away2.at[d], land.at[far], me_r, me_c).wait_recv()
    for copy in pending:
        copy.wait_send()


def solve(n_row, n_col, neighbours, right_side, anchor, owners, row_offset, col_offset, tiles):
    n_blk, fan, side, _ = tiles.shape
    rows = 2 * n_blk
    q_all = n_blk * fan * 8 + n_blk * 8
    vmem = pl.BlockSpec(memory_space=pltpu.VMEM)
    dma = pltpu.SemaphoreType.DMA
    return pl.pallas_call(
        functools.partial(solve_kernel, n_row, n_col),
        name="solve_and_route",
        out_shape=(
            jax.ShapeDtypeStruct(right_side.shape, F32),
            jax.ShapeDtypeStruct((n_col, n_row, 1, 128), F32),
        ),
        in_specs=[pl.BlockSpec(memory_space=pltpu.SMEM)] + [vmem] * 5 + [pl.BlockSpec(memory_space=pl.ANY)],
        out_specs=(vmem, vmem),
        scratch_shapes=[
            pltpu.VMEM(tiles.shape, F32),
            pltpu.VMEM(tiles.shape, BF16),
            pltpu.VMEM(tiles.shape, BF16),
            pltpu.VMEM((3, side, side), F32),
            pltpu.VMEM((q_all, 3 * side), BF16),
            pltpu.VMEM((side, 384), BF16),
            pltpu.VMEM((q_all, side), F32),
            pltpu.VMEM((384, side), F32),
            pltpu.VMEM((3, 9 * rows, side), F32),
            pltpu.VMEM((3, 9, rows, side), F32),
            pltpu.VMEM((3, n_row, 8, 128), F32),
            pltpu.VMEM((3, n_col, 8, 128), F32),
            pltpu.VMEM((n_blk, n_row * n_col, side), BF16),
            pltpu.VMEM((n_blk, side), F32),
            pltpu.VMEM((n_row, n_col, 1, 128), F32),
            pltpu.VMEM((n_col, n_row, 1, 128), F32),
            dma((n_blk,)),
            dma((3, 9)), dma((3, 9)), dma((3, 9)), dma((3, 9)),
            dma((3, n_row)), dma((3, n_row)), dma((3, n_col)), dma((3, n_col)),
            dma((n_row,)), dma((n_row,)), dma((n_col,)), dma((n_col,)), dma((2,)),
        ],
        compiler_params=pltpu.CompilerParams(
            collective_id=0, has_side_effects=True, vmem_limit_bytes=48 * 2**20
        ),
        cost_estimate=pl.CostEstimate(flops=10**9, bytes_accessed=2**23, transcendentals=0),
    )(neighbours, right_side, anchor, owners, row_offset, col_offset, tiles)


def edge_kernel(n_row, n_col, top_ref, bottom_ref, left_ref, right_ref, up_ref, down_ref, west_ref, east_ref, ss, rs):
    me_r = lax.axis_index("row")
    me_c = lax.axis_index("col")
    barrier = pltpu.get_barrier_semaphore()

    def at(dr, dc):
        return lax.rem(me_r + dr + n_row, n_row), lax.rem(me_c + dc + n_col, n_col)

    for g, (dr, dc) in enumerate(AROUND):
        if g != 4:
            row, col = at(dr, dc)
            pl.semaphore_signal(barrier, inc=1, device_id={"row": row, "col": col}, device_id_type=MESH)
    pl.semaphore_wait(barrier, 8)
    length = left_ref.shape[1]
    first = (slice(None), pl.ds(0, 128))
    last = (slice(None), pl.ds(length - 128, 128))
    inner = (slice(None), pl.ds(128, length))
    above = (slice(None), pl.ds(0, 128))
    below = (slice(None), pl.ds(length + 128, 128))
    plan = {
        (-1, 0): (top_ref, down_ref),
        (1, 0): (bottom_ref, up_ref),
        (0, -1): (left_ref, east_ref.at[inner]),
        (0, 1): (right_ref, west_ref.at[inner]),
        (-1, -1): (left_ref.at[first], east_ref.at[below]),
        (-1, 1): (right_ref.at[first], west_ref.at[below]),
        (1, -1): (left_ref.at[last], east_ref.at[above]),
        (1, 1): (right_ref.at[last], west_ref.at[above]),
    }
    copies = []
    for g, side in enumerate(AROUND):
        if g != 4:
            src, dst = plan[side]
            row, col = at(*side)
            copy = remote(src, dst, ss.at[g], rs.at[g], row, col)
            copy.start()
            copies.append(copy)
    for copy in copies:
        copy.wait_recv()
    for copy in copies:
        copy.wait_send()


def exchange_edges(n_row, n_col, top, bottom, left, right):
    vmem = pl.BlockSpec(memory_space=pltpu.VMEM)
    length, width = left.shape[1], top.shape[1]
    return pl.pallas_call(
        functools.partial(edge_kernel, n_row, n_col),
        name="grid_edges",
        out_shape=(
            jax.ShapeDtypeStruct((8, width), F32),
            jax.ShapeDtypeStruct((8, width), F32),
            jax.ShapeDtypeStruct((8, length + 256), F32),
            jax.ShapeDtypeStruct((8, length + 256), F32),
        ),
        in_specs=[vmem] * 4,
        out_specs=(vmem,) * 4,
        scratch_shapes=[pltpu.SemaphoreType.DMA((9,)), pltpu.SemaphoreType.DMA((9,))],
        compiler_params=pltpu.CompilerParams(collective_id=1, has_side_effects=True),
    )(top, bottom, left, right)


CHUNK = 128
STRIP = 64


def diffuse_kernel(n_row, n_col, field_ref, up_ref, down_ref, west_ref, east_ref, out_ref, one, two, in_sem, out_sem):
    length, width = field_ref.shape
    wide = width + 128
    n_chunk = length // CHUNK
    me_r = lax.axis_index("row")
    me_c = lax.axis_index("col")

    def load(i):
        return pltpu.make_async_copy(
            field_ref.at[pl.ds(i * CHUNK, CHUNK)], one.at[pl.ds(8 + i * CHUNK, CHUNK), pl.ds(0, width)], in_sem.at[i]
        )

    for i in range(n_chunk):
        load(i).start()
    not_first_row = (me_r > 0).astype(F32)
    not_last_row = (me_r < n_row - 1).astype(F32)
    not_first_col = (me_c > 0).astype(F32)
    not_last_col = (me_c < n_col - 1).astype(F32)
    lane = iota((1, 128), 1)
    keep_lane = jnp.where(lane < 8, not_last_col, jnp.where(lane >= 120, not_first_col, 0.0))
    one[0:8, 0:width] = up_ref[...] * not_first_row
    one[length + 8:length + 16, 0:width] = down_ref[...] * not_last_row
    gap = jnp.zeros((112, 128), F32)
    for i in range(length // 128 + 2):
        here = pl.ds(i * 128, 128)
        tile = jnp.transpose(jnp.concatenate([east_ref[:, here], gap, west_ref[:, here]], axis=0)) * keep_lane
        if i == 0:
            one[0:8, width:wide] = tile[120:128] * not_first_row
        elif i == length // 128 + 1:
            one[length + 8:length + 16, width:wide] = tile[0:8] * not_last_row
        else:
            one[8 + (i - 1) * 128:8 + i * 128, width:wide] = tile
    for i in range(n_chunk):
        load(i).wait()

    keep_cols = jnp.concatenate([jnp.ones((1, width), F32), keep_lane], axis=1)

    def summed(src, start, n):
        window = src[pl.ds(pl.multiple_of(start - 8, 8), n + 16), :]
        centre = window[8:8 + n]
        above = window[7:7 + n]
        below = window[9:9 + n]
        return (centre + above) + (below + pltpu.roll(centre, 1, 1)) + pltpu.roll(centre, wide - 1, 1)

    def edge(src, dst):
        for start, keep in ((0, not_first_row), (length + 8, not_last_row)):
            c = src[start:start + 8, :]
            if start == 0:
                above = pltpu.roll(c, 1, 0)
                below = src[1:9, :]
            else:
                above = src[start - 1:start + 7, :]
                below = pltpu.roll(c, 7, 0)
            total = c + above + below + pltpu.roll(c, 1, 1) + pltpu.roll(c, wide - 1, 1)
            dst[start:start + 8, :] = total * keep_cols * keep

    src, dst = one, two
    for step in range(STEPS):
        if step < STEPS - 1:
            edge(src, dst)

            def strip(i, carry, src=src, dst=dst):
                start = pl.multiple_of(8 + i * STRIP, 8)
                total = summed(src, start, STRIP)
                dst[pl.ds(start, STRIP), 0:width] = total[:, 0:width]
                dst[pl.ds(start, STRIP), width:wide] = total[:, width:wide] * keep_lane
                return carry

            lax.fori_loop(0, length // STRIP, strip, 0)
        else:

            def strip(i, carry, src=src, dst=dst):
                start = pl.multiple_of(8 + i * STRIP, 8)
                total = summed(src, start, STRIP)
                dst[pl.ds(start, STRIP), 0:width] = total[:, 0:width] * (0.2 ** STEPS)
                return carry

            for i in range(n_chunk):
                lax.fori_loop(i * (CHUNK // STRIP), (i + 1) * (CHUNK // STRIP), strip, 0)
                store_chunk(dst, out_ref, out_sem, i, width).start()
        src, dst = dst, src
    for i in range(n_chunk):
        store_chunk(src, out_ref, out_sem, i, width).wait()


def store_chunk(buf, out_ref, out_sem, i, width):
    return pltpu.make_async_copy(
        buf.at[pl.ds(8 + i * CHUNK, CHUNK), pl.ds(0, width)], out_ref.at[pl.ds(i * CHUNK, CHUNK)], out_sem.at[i]
    )


def diffuse(n_row, n_col, field, up, down, west, east):
    length, width = field.shape
    vmem = pl.BlockSpec(memory_space=pltpu.VMEM)
    hbm = pl.BlockSpec(memory_space=pl.ANY)
    n_chunk = length // CHUNK
    return pl.pallas_call(
        functools.partial(diffuse_kernel, n_row, n_col),
        name="diffuse",
        out_shape=jax.ShapeDtypeStruct(field.shape, F32),
        in_specs=[hbm] + [vmem] * 4,
        out_specs=hbm,
        scratch_shapes=[
            pltpu.VMEM((length + 16, width + 128), F32),
            pltpu.VMEM((length + 16, width + 128), F32),
            pltpu.SemaphoreType.DMA((n_chunk,)),
            pltpu.SemaphoreType.DMA((n_chunk,)),
        ],
        compiler_params=pltpu.CompilerParams(vmem_limit_bytes=32 * 2**20),
        cost_estimate=pl.CostEstimate(flops=4 * 5 * length * width, bytes_accessed=8 * length * width, transcendentals=0),
    )(field, up, down, west, east)


def per_device(right_side, anchor, tiles, neighbours, owners, row_offset, col_offset, macro_density):
    n_blk, _, side, _ = tiles.shape[0], tiles.shape[1], tiles.shape[2], tiles.shape[3]
    n_row, n_col = lax.axis_size("row"), lax.axis_size("col")
    solution, arrived = solve(
        n_row, n_col, neighbours, right_side, anchor, owners.reshape(n_blk, side),
        row_offset.reshape(n_blk, side), col_offset.reshape(n_blk, side), tiles,
    )
    arrived = arrived.reshape(n_row * n_col, 128)
    at_row = arrived[:, :CAP].reshape(-1)
    at_col = arrived[:, CAP:2 * CAP].reshape(-1)
    grid_rows, grid_cols = macro_density.shape

    def window_of(position, limit):
        start_cell = jnp.clip(jnp.floor(position).astype(jnp.int32) - 7, 0, limit - 16)
        cells = lax.iota(jnp.int32, limit)[None, :]
        inside = ((cells >= start_cell[:, None]) & (cells < start_cell[:, None] + 16)).astype(F32)
        offset = cells.astype(F32) - position[:, None]
        return (jnp.exp(-0.5 * offset * offset) * inside).astype(BF16)

    spread = lax.dot_general(
        window_of(at_row, grid_rows), window_of(at_col, grid_cols), (((0,), (0,)), ((), ())), preferred_element_type=F32
    )
    field = macro_density + spread
    edges = exchange_edges(
        n_row, n_col, field[:8], field[-8:], field[:, :8].T, field[:, -8:].T
    )
    return solution, diffuse(n_row, n_col, field, *edges)


def solution(mesh):
    blocks = P(("row", "col"))
    return jax.shard_map(
        per_device,
        mesh=mesh,
        in_specs=(
            P(("row", "col"), None, None),
            P(("row", "col"), None),
            P(("row", "col"), None, None, None),
            P(("row", "col"), None),
            P(("row", "col"), None),
            blocks,
            blocks,
            P("row", "col"),
        ),
        out_specs=(P(("row", "col"), None, None), P("row", "col")),
        check_vma=False,
    )
```

time: 739 us -> 148 us (0.20)
  the two profiles are of different devices: /device:TPU:34 before, /device:TPU:1 now
where the time goes in v1:
time: 148 us
  Pallas kernels  108 us (73%)
  matrix products  22 us (15%)
  local copies, waits for them, and re-layouts  15.2 us (10%)
    pallas_call x1, Pallas kernels, solve(): pl.pallas_call(functools.partial(solve_kernel, n_row, n_col), name='solve...  76.3 us
    dot_general x1, matrix products, per_device(): lax.dot_general(window_of(at_row, grid_rows), window_of(at_col, grid_cols...  22 us
    pallas_call x1, Pallas kernels, diffuse(): pl.pallas_call(functools.partial(diffuse_kernel, n_row, n_col), name='dif...  21.6 us
    unnamed x19, local copies, waits for them, and re-layouts  10.7 us
    pallas_call x1, Pallas kernels, exchange_edges(): pl.pallas_call(functools.partial(edge_kernel, n_row, n_col), name='grid_e...  10.5 us

profile of v1, /device:TPU:1, one launch (start us, length us, event | category | flops | bytes accessed | tf_op | source)
XLA Modules:
  0.0 147.6 jit_solution(3582079735113140649)
XLA Ops:
  0.6 0.8 copy.13.nbr_ref
  1.4 0.5 broadcast.91
  1.9 1.4 reduce.3
  3.3 0.7 reshape.61.roff_ref
  4.0 0.7 reshape.62.coff_ref
  4.7 0.0 copy-start.4
  4.7 0.7 copy-done.4
  5.4 0.0 copy-start.7
  5.4 0.7 copy-done.7
  6.1 76.3 %solve_and_route.1 = (f32[8,2,256]{2,1,0:T(2,128)S(1)}, f32[16,8,1,128]{3,2,1,0:T(1,128)S(1)}) custom-call(s32[8,4]{1,0:T(8,128)S(1)} %copy.13.nbr_ref, f32[8,2,256]{2,1,0:T(2,128)S(1)} %copy-done.4, f32[8,256]{1,0:T(8,128)S(1)} %copy-done.7, s32[8,256]{1,0:T(8,128)S(1)} %reshape.60.owner_ref, s32[8,256]{1,0:T(8,128)S(1)} %reshape.61.roff_ref, ...), custom_call_target="tpu_custom_call" | custom-call | flops 1000000000 | bytes 8388608 | tf_op jit(solution)/shard_map/solve_and_route/pallas_call | solution.py:327
  82.4 0.1 fusion.25
  82.5 0.1 reshape.64
  82.6 0.1 reshape.65
  82.7 22.0 %fusion.17.field_ref = f32[2048,512]{1,0:T(8,128)S(1)} fusion(f32[2048,512]{1,0:T(8,128)} %param.15, f32[4096]{0:T(1024)S(1)} %reshape.65, f32[512]{0:T(512)S(1)} %iota_convert_fusion.1, s32[4096]{0:T(1024)S(1)} %get-tuple-element.23, s32[4096]{0:T(1024)S(1)} %get-tuple-element.22, f32[4096]{0:T(1024)S(1)} %reshape.64, f32[2048]{0:T(1024)S(1)} %iota_convert_fusion, ...), kind=kOutput, calls=%fused_computation.21 | convolution fusion | flops 8674869248 | bytes 8497152 | tf_op jit(solution)/shard_map/dot_general | solution.py:563
  104.7 0.6 fusion.24
  105.3 0.4 slice_bitcast_fusion
  105.6 0.0 copy-start
  105.7 2.0 %copy-done = f32[2048,512]{1,0:T(8,128)} copy-done((f32[2048,512]{1,0:T(8,128)}, f32[2048,512]{1,0:T(8,128)S(1)}, u32[]{:S(2)}) %copy-start) | copy-done | bytes 4194328
  107.7 0.9 copy.15.right_ref
  108.6 0.9 copy.14.left_ref
  109.5 10.5 %grid_edges.1 = (f32[8,512]{1,0:T(8,128)}, f32[8,512]{1,0:T(8,128)}, f32[8,2304]{1,0:T(8,128)}, f32[8,2304]{1,0:T(8,128)}) custom-call(f32[8,512]{1,0:T(8,128)} %get-tuple-element.17.top_ref, f32[8,512]{1,0:T(8,128)} %get-tuple-element.16.bottom_ref, f32[8,2048]{1,0:T(8,128)} %copy.14.left_ref, f32[8,2048]{1,0:T(8,128)} %copy.15.right_ref), custom_call_target="tpu_custom_call" | custom-call | tf_op jit(solution)/shard_map/grid_edges/pallas_call | solution.py:411
  120.0 0.0 copy-start.1
  120.0 2.2 %copy-done.1 = f32[2048,512]{1,0:T(8,128)S(1)} copy-done((f32[2048,512]{1,0:T(8,128)S(1)}, f32[2048,512]{1,0:T(8,128)}, u32[]{:S(2)}) %copy-start.1) | copy-done | bytes 4194328
  122.2 0.0 copy-start.2
  122.2 0.9 copy-done.2
  123.1 0.0 copy-start.3
  123.1 0.9 copy-done.3
  124.0 0.0 copy-start.5
  124.0 0.7 copy-done.5
  124.7 0.0 copy-start.6
  124.7 0.7 copy-done.6
  125.4 21.6 %diffuse.1 = f32[2048,512]{1,0:T(8,128)} custom-call(f32[2048,512]{1,0:T(8,128)S(1)} %copy-done.1, f32[8,512]{1,0:T(8,128)S(1)} %copy-done.5, f32[8,512]{1,0:T(8,128)S(1)} %copy-done.6, f32[8,2304]{1,0:T(8,128)S(1)} %copy-done.2, f32[8,2304]{1,0:T(8,128)S(1)} %copy-done.3), custom_call_target="tpu_custom_call" | custom-call | flops 20971520 | bytes 8388608 | tf_op jit(solution)/shard_map/diffuse/pallas_call | solution.py:527
  147.0 0.6 copy.17
  (4 shorter events, 0.0 us)
Async XLA Ops:
  4.7 0.7 copy-start.4
  5.4 0.7 copy-start.7
  105.6 2.0 %copy-start = (f32[2048,512]{1,0:T(8,128)}, f32[2048,512]{1,0:T(8,128)S(1)}, u32[]{:S(2)}) copy-start(f32[2048,512]{1,0:T(8,128)S(1)} %fusion.17.field_ref) | copy-start | bytes 12582916
  120.0 2.2 %copy-start.1 = (f32[2048,512]{1,0:T(8,128)S(1)}, f32[2048,512]{1,0:T(8,128)}, u32[]{:S(2)}) copy-start(f32[2048,512]{1,0:T(8,128)} %copy-done) | copy-start | bytes 12582916
  122.2 0.9 copy-start.2
  123.1 0.9 copy-start.3
  124.0 0.7 copy-start.5
  124.7 0.7 copy-start.6

commit v2 on v1

--- a/solution.py
+++ b/solution.py
@@ -46,9 +46,9 @@
 def solve_kernel(
     n_row, n_col,
     nbr_ref, rhs_ref, anchor_ref, owner_ref, roff_ref, coff_ref, tiles_ref,
-    sol_ref, arrived_ref,
+    sol_ref, pos_ref,
     stage, thi, tlo, xbuf, sel, spread_sel, gath, terms, back, recv,
-    ar_row, ar_col, own_hot, rank_sc, out_rows, mid_rows,
+    ar_row, ar_col, own_hot, rank_sc, weight_sc, out_rows, mid_rows, end_rows, table_sc,
     tile_sem, fs, fr, bs, br, rs, rr, cs, cr, away1, got, away2, land, keep_sem,
 ):
     n_blk, fan, side, _ = thi.shape
@@ -58,13 +58,16 @@
     n_dev = n_row * n_col
     me_r = lax.axis_index("row")
     me_c = lax.axis_index("col")
+    row_order = sorted(range(1, n_row), key=lambda d: -min(d, n_row - d))
+    col_order = sorted(range(1, n_col), key=lambda d: -(min(d // 4, 4 - d // 4) + min(d % 4, 4 - d % 4)))
+    around = sorted((g for g in range(9) if g != 4), key=lambda g: -abs(AROUND[g][0]) - 2 * abs(AROUND[g][1]))
 
     for b in range(n_blk):
         pltpu.make_async_copy(tiles_ref.at[b], stage.at[b], tile_sem.at[b]).start()
 
     barrier = pltpu.get_barrier_semaphore()
-    peers = [(d, 0) for d in range(1, n_row)] + [(0, d) for d in range(1, n_col)]
-    peers += [(dr, dc) for dr, dc in AROUND if dr and dc]
+    peers = [AROUND[g] for g in around if AROUND[g][0] and AROUND[g][1]]
+    peers += [(0, d) for d in col_order] + [(d, 0) for d in row_order]
     for dr, dc in peers:
         pl.semaphore_signal(
             barrier, inc=1,
@@ -79,6 +82,18 @@
     for b in range(n_blk):
         xbuf[0, own_lo + 2 * b:own_lo + 2 * b + 2, :] = rhs_ref[b]
 
+    upper = (iota((side, side), 0) < iota((side, side), 1)).astype(F32).astype(BF16)
+    count = jnp.zeros((n_dev, 1), F32)
+    held = jnp.zeros((1, n_dev), F32)
+    for b in range(n_blk):
+        hot = (owner_ref[b:b + 1, :] == iota((n_dev, side), 0)).astype(F32)
+        before = nn_dot(hot.astype(BF16), upper) + count
+        rank_sc[b:b + 1, :] = jnp.sum(hot * before, axis=0, keepdims=True)
+        count = count + jnp.sum(hot, axis=1, keepdims=True)
+        turned = jnp.transpose(hot)
+        own_hot[b] = turned.astype(BF16)
+        held = held + jnp.sum(turned, axis=0, keepdims=True)
+
     pl.semaphore_wait(barrier, len(peers))
 
     def x_rows(it, g):
@@ -87,9 +102,8 @@
     pending = []
 
     def forward(it):
-        for g, (dr, dc) in enumerate(AROUND):
-            if g == 4:
-                continue
+        for g in around:
+            dr, dc = AROUND[g]
             copy = remote(
                 x_rows(it, 4), x_rows(it, 8 - g), fs.at[it, g], fr.at[it, 8 - g],
                 lax.rem(me_r + dr + n_row, n_row), lax.rem(me_c + dc + n_col, n_col),
@@ -98,14 +112,12 @@
             pending.append(copy)
 
     def forward_wait(it):
-        for g in range(9):
-            if g != 4:
-                remote(x_rows(it, 4), x_rows(it, g), fs.at[it, g], fr.at[it, g], me_r, me_c).wait_recv()
+        for g in around:
+            remote(x_rows(it, 4), x_rows(it, g), fs.at[it, g], fr.at[it, g], me_r, me_c).wait_recv()
 
     def backward(it):
-        for g, (dr, dc) in enumerate(AROUND):
-            if g == 4:
-                continue
+        for g in around:
+            dr, dc = AROUND[g]
             copy = remote(
                 back.at[it, pl.ds(g * rows, rows)], recv.at[it, 8 - g], bs.at[it, g], br.at[it, 8 - g],
                 lax.rem(me_r + dr + n_row, n_row), lax.rem(me_c + dc + n_col, n_col),
@@ -114,9 +126,8 @@
             pending.append(copy)
 
     def backward_wait(it):
-        for g in range(9):
-            if g != 4:
-                remote(back.at[it, pl.ds(g * rows, rows)], recv.at[it, g], bs.at[it, g], br.at[it, g], me_r, me_c).wait_recv()
+        for g in around:
+            remote(back.at[it, pl.ds(g * rows, rows)], recv.at[it, g], bs.at[it, g], br.at[it, g], me_r, me_c).wait_recv()
 
     forward(0)
 
@@ -141,16 +152,6 @@
     sel_t = sel[:, 0:side].astype(F32) + sel[:, side:2 * side].astype(F32) + sel[:, 2 * side:].astype(F32)
     spread_sel[...] = jnp.transpose(jnp.concatenate([sel_t, jnp.zeros((384 - q_all, side), F32)], axis=0)).astype(BF16)
     terms[...] = jnp.zeros_like(terms)
-
-    upper = (iota((side, side), 0) < iota((side, side), 1)).astype(F32).astype(BF16)
-
-    count = jnp.zeros((n_dev, 1), F32)
-    for b in range(n_blk):
-        hot = (owner_ref[b:b + 1, :] == iota((n_dev, side), 0)).astype(F32)
-        own_hot[b] = hot.astype(BF16)
-        before = nn_dot(hot.astype(BF16), upper) + count
-        rank_sc[b:b + 1, :] = jnp.sum(hot * before, axis=0, keepdims=True)
-        count = count + jnp.sum(hot, axis=1, keepdims=True)
 
     def split_block(b, carry):
         pltpu.make_async_copy(tiles_ref.at[b], stage.at[b], tile_sem.at[b]).wait()
@@ -182,6 +183,8 @@
                 down = nn_dot(own_b, thi[b, k]) + nn_dot(own_b, tlo[b, k])
                 terms[pl.ds(q, 8), :] = down[6:7, :] * far - down
             weight = total[6:7, :] + anchor_ref[pl.ds(b, 1), :]
+            if it == 0:
+                weight_sc[pl.ds(b, 1), :] = weight
             terms[pl.ds(pl.multiple_of(q_own + b * 8, 8), 8), :] = weight * own - total
             return carry
 
@@ -199,15 +202,17 @@
                 image = image + recv[it, g]
         return image
 
-    def dots_start(it, pairs):
+    def dots_start(it, pairs, more=None):
         lane = iota((8, 128), 1)
         tile = jnp.zeros((8, 128), F32)
         for d, (a, b) in enumerate(pairs):
             e = a * b
             e = e[0:8] + e[8:16]
+            if d == 0 and more is not None:
+                e = e + more
             tile = jnp.where(lane == d, jnp.sum(e, axis=1, keepdims=True), tile)
         ar_row[it, me_r] = tile
-        for d in range(1, n_row):
+        for d in row_order:
             copy = remote(
                 ar_row.at[it, me_r], ar_row.at[it, me_r], rs.at[it, d], rr.at[it, me_r],
                 lax.rem(me_r + d, n_row), me_c,
@@ -216,11 +221,11 @@
             pending.append(copy)
 
     def dots_middle(it):
-        for d in range(1, n_row):
+        for d in row_order:
             far = lax.rem(me_r + d, n_row)
             remote(ar_row.at[it, far], ar_row.at[it, far], rs.at[it, d], rr.at[it, far], me_r, me_c).wait_recv()
         ar_col[it, me_c] = jnp.sum(ar_row[it], axis=0)
-        for d in range(1, n_col):
+        for d in col_order:
             copy = remote(
                 ar_col.at[it, me_c], ar_col.at[it, me_c], cs.at[it, d], cr.at[it, me_c],
                 me_r, lax.rem(me_c + d, n_col),
@@ -229,7 +234,7 @@
             pending.append(copy)
 
     def dots_end(it, n):
-        for d in range(1, n_col):
+        for d in col_order:
             far = lax.rem(me_c + d, n_col)
             remote(ar_col.at[it, far], ar_col.at[it, far], cs.at[it, d], cr.at[it, far], me_r, me_c).wait_recv()
         t = jnp.sum(ar_col[it], axis=0)
@@ -238,7 +243,7 @@
         return [t[:, d:d + 1] for d in range(n)]
 
     def times(c, v):
-        return jnp.concatenate([c] * (rows // 8), axis=0) * v
+        return jnp.concatenate([c] * (v.shape[0] // 8), axis=0) * v
 
     r0 = xbuf[0, own_lo:own_lo + rows, :]
     apply(0)
@@ -255,65 +260,110 @@
     forward(2)
     r1 = r0 - times(alpha0, w0)
     dots_start(1, [(r1, r1), (r1, w1), (r1, w0)])
-    apply(2, lambda: dots_middle(1))
+
+    rank_of = iota((CAP, side), 0)
+    table = jnp.zeros((8 * CAP, n_dev), F32)
+    for b in range(n_blk):
+        mine = rank_of == rank_sc[b:b + 1, :].astype(jnp.int32)
+        values = [v[2 * b + c:2 * b + c + 1, :] for v in (r0, w0, w1) for c in (0, 1)]
+        values += [roff_ref[b:b + 1, :].astype(F32), coff_ref[b:b + 1, :].astype(F32)]
+        placed = jnp.concatenate([jnp.where(mine, v, 0.0) for v in values], axis=0)
+        for part in split3(placed):
+            table = table + nn_dot(part, own_hot[b])
+    empty = iota((CAP, n_dev), 0).astype(F32) >= held
+    table = jnp.concatenate(
+        [table[0:6 * CAP], jnp.where(empty, NONE, table[6 * CAP:7 * CAP]), table[7 * CAP:]], axis=0
+    )
+    table = jnp.transpose(table)
+    for o in range(n_dev):
+        out_rows[o // n_col, o % n_col] = table[o:o + 1, :]
+    keep = pltpu.make_async_copy(out_rows.at[me_r], mid_rows.at[:, me_r], keep_sem.at[0])
+    keep.start()
+    for d in row_order:
+        far = lax.rem(me_r + d, n_row)
+        copy = remote(out_rows.at[far], mid_rows.at[:, me_r], away1.at[d], got.at[me_r], far, me_c)
+        copy.start()
+        pending.append(copy)
+
+    dots_middle(1)
+
+    keep.wait()
+    for d in row_order:
+        far = lax.rem(me_r + d, n_row)
+        remote(out_rows.at[far], mid_rows.at[:, far], away1.at[d], got.at[far], me_r, me_c).wait_recv()
+    keep2 = pltpu.make_async_copy(mid_rows.at[me_c], end_rows.at[me_c], keep_sem.at[1])
+    keep2.start()
+    for d in col_order:
+        far = lax.rem(me_c + d, n_col)
+        copy = remote(mid_rows.at[far], end_rows.at[me_c], away2.at[d], land.at[me_c], me_r, far)
+        copy.start()
+        pending.append(copy)
+
+    forward_wait(2)
     gamma1, r1w1, r1w0 = dots_end(1, 3)
     beta0 = gamma1 / gamma0
     curve1 = r1w1 + 2.0 * beta0 * r1w0 + beta0 * beta0 * curve0
     alpha1 = gamma1 / curve1
     p1 = r1 + times(beta0, r0)
     s1 = w1 + times(beta0, w0)
-    z1 = applied(2)
-    q1 = z1 + times(beta0, z0)
     r2 = r1 - times(alpha1, s1)
-    w2 = w1 - times(alpha1, q1)
-    dots_start(2, [(r2, r2), (r2, w2), (r2, s1)])
+
+    near_w0 = xbuf[1, 0:9 * rows, :]
+    near_r1 = xbuf[0, 0:9 * rows, :] - times(alpha0, near_w0)
+    near_r2 = near_r1 - times(alpha1, xbuf[2, 0:9 * rows, :] + times(beta0, near_w0))
+    near_r2 = jnp.concatenate([near_r2, jnp.where(below == 0, 1.0, 0.0)], axis=0)
+    gath[...] = nn_dot(sel[...], jnp.concatenate(split3(near_r2), axis=0))
+
+    def energy_block(b, carry):
+        own_b = gath[pl.ds(pl.multiple_of(q_own + b * 8, 8), 8), :].astype(BF16)
+        for k in range(fan):
+            q = pl.multiple_of((b * fan + k) * 8, 8)
+            down = nn_dot(own_b, thi[b, k]) + nn_dot(own_b, tlo[b, k])
+            terms[pl.ds(q, 8), :] = down[6:7, :] * gath[pl.ds(q, 8), :] - 2.0 * down
+        return carry
+
+    lax.fori_loop(0, n_blk, energy_block, 0)
+
+    def over_parts(v):
+        return v + pltpu.roll(v, q_own - 2, 0) + pltpu.roll(v, q_own - 4, 0)
+
+    cross = over_parts(terms[0:q_own, :]) * over_parts(gath[0:q_own, :])
+    cross = jnp.sum(cross.reshape(q_own // 8, 8, side), axis=0)
+    cross = jnp.where(iota((8, side), 0) < 2, cross, 0.0)
+    weights = weight_sc[...]
+    weights = jnp.concatenate([weights[b:b + 1] for b in range(n_blk) for _ in (0, 1)], axis=0)
+    dots_start(2, [(r2, weights * r2), (r2, r2), (r2, s1)], more=cross)
+
+    keep2.wait()
+    for d in col_order:
+        far = lax.rem(me_c + d, n_col)
+        remote(mid_rows.at[far], end_rows.at[far], away2.at[d], land.at[far], me_r, me_c).wait_recv()
     dots_middle(2)
-    gamma2, r2w2, r2s1 = dots_end(2, 3)
+    for o in range(n_dev):
+        table_sc[o:o + 1, :] = end_rows[o // n_row, o % n_row]
+    curve_r2, gamma2, r2s1 = dots_end(2, 3)
     beta1 = gamma2 / gamma1
-    curve2 = r2w2 + 2.0 * beta1 * r2s1 + beta1 * beta1 * curve1
+    curve2 = curve_r2 + 2.0 * beta1 * r2s1 + beta1 * beta1 * curve1
     alpha2 = gamma2 / curve2
+
+    of_b = alpha0 + alpha1 * (1.0 + beta0) + alpha2 * (1.0 + beta1 * (1.0 + beta0))
+    of_w0 = -alpha1 * alpha0 - alpha2 * (alpha0 + alpha1 * beta0 + beta1 * alpha0)
+    of_w1 = -alpha2 * alpha1
+    lane = iota((1, 128), 1)
+
+    def by_lane(first, second):
+        return jnp.where(
+            lane < CAP, first[0:1], jnp.where(lane < 2 * CAP, first[1:2], jnp.where(lane < 3 * CAP, second[0:1], second[1:2]))
+        )
+
+    near = table_sc[:, 0:128] * by_lane(of_b, of_w0)
+    far = table_sc[:, 128:256]
+    moved = near + pltpu.roll(near, 64, 1) + far * by_lane(of_w1, of_w1)
+    pos_ref[...] = pltpu.roll(far, 64, 1) + 3.0 * jnp.tanh(moved)
+
     x = times(alpha0, r0) + times(alpha1, p1) + times(alpha2, r2 + times(beta1, p1))
     for b in range(n_blk):
         sol_ref[b] = x[2 * b:2 * b + 2, :]
-
-    moved = 3.0 * jnp.tanh(x)
-    table = jnp.zeros((n_dev, 128), F32)
-    lane_rank = iota((2 * CAP, side), 0)
-    for b in range(n_blk):
-        pos_row = roff_ref[b:b + 1, :].astype(F32) + moved[2 * b:2 * b + 1, :]
-        pos_col = coff_ref[b:b + 1, :].astype(F32) + moved[2 * b + 1:2 * b + 2, :]
-        rank = rank_sc[b:b + 1, :].astype(jnp.int32)
-        placed = jnp.where(lane_rank == rank, pos_row, jnp.where(lane_rank == rank + CAP, pos_col, 0.0))
-        placed = jnp.concatenate([placed, jnp.zeros((128 - 2 * CAP, side), F32)], axis=0)
-        for part in split3(placed):
-            table = table + nt_dot(own_hot[b], part)
-    lane_of = lax.rem(iota((n_dev, 128), 1), CAP).astype(F32)
-    table = jnp.where(lane_of < count, table, NONE)
-    for o in range(n_dev):
-        out_rows[o // n_col, o % n_col] = table[o:o + 1, :]
-
-    keep = pltpu.make_async_copy(out_rows.at[me_r], mid_rows.at[:, me_r], keep_sem.at[0])
-    keep.start()
-    for d in range(1, n_row):
-        far = lax.rem(me_r + d, n_row)
-        copy = remote(out_rows.at[far], mid_rows.at[:, me_r], away1.at[d], got.at[me_r], far, me_c)
-        copy.start()
-        pending.append(copy)
-    keep.wait()
-    for d in range(1, n_row):
-        far = lax.rem(me_r + d, n_row)
-        remote(out_rows.at[far], mid_rows.at[:, far], away1.at[d], got.at[far], me_r, me_c).wait_recv()
-    keep2 = pltpu.make_async_copy(mid_rows.at[me_c], arrived_ref.at[me_c], keep_sem.at[1])
-    keep2.start()
-    for d in range(1, n_col):
-        far = lax.rem(me_c + d, n_col)
-        copy = remote(mid_rows.at[far], arrived_ref.at[me_c], away2.at[d], land.at[me_c], me_r, far)
-        copy.start()
-        pending.append(copy)
-    keep2.wait()
-    for d in range(1, n_col):
-        far = lax.rem(me_c + d, n_col)
-        remote(mid_rows.at[far], arrived_ref.at[far], away2.at[d], land.at[far], me_r, me_c).wait_recv()
     for copy in pending:
         copy.wait_send()
 
@@ -321,6 +371,7 @@
 def solve(n_row, n_col, neighbours, right_side, anchor, owners, row_offset, col_offset, tiles):
     n_blk, fan, side, _ = tiles.shape
     rows = 2 * n_blk
+    n_dev = n_row * n_col
     q_all = n_blk * fan * 8 + n_blk * 8
     vmem = pl.BlockSpec(memory_space=pltpu.VMEM)
     dma = pltpu.SemaphoreType.DMA
@@ -329,7 +380,7 @@
         name="solve_and_route",
         out_shape=(
             jax.ShapeDtypeStruct(right_side.shape, F32),
-            jax.ShapeDtypeStruct((n_col, n_row, 1, 128), F32),
+            jax.ShapeDtypeStruct((n_dev, 128), F32),
         ),
         in_specs=[pl.BlockSpec(memory_space=pltpu.SMEM)] + [vmem] * 5 + [pl.BlockSpec(memory_space=pl.ANY)],
         out_specs=(vmem, vmem),
@@ -342,14 +393,17 @@
             pltpu.VMEM((side, 384), BF16),
             pltpu.VMEM((q_all, side), F32),
             pltpu.VMEM((384, side), F32),
-            pltpu.VMEM((3, 9 * rows, side), F32),
-            pltpu.VMEM((3, 9, rows, side), F32),
+            pltpu.VMEM((2, 9 * rows, side), F32),
+            pltpu.VMEM((2, 9, rows, side), F32),
             pltpu.VMEM((3, n_row, 8, 128), F32),
             pltpu.VMEM((3, n_col, 8, 128), F32),
-            pltpu.VMEM((n_blk, n_row * n_col, side), BF16),
+            pltpu.VMEM((n_blk, side, n_dev), BF16),
             pltpu.VMEM((n_blk, side), F32),
-            pltpu.VMEM((n_row, n_col, 1, 128), F32),
-            pltpu.VMEM((n_col, n_row, 1, 128), F32),
+            pltpu.VMEM((n_blk, side), F32),
+            pltpu.VMEM((n_row, n_col, 1, 8 * CAP), F32),
+            pltpu.VMEM((n_col, n_row, 1, 8 * CAP), F32),
+            pltpu.VMEM((n_col, n_row, 1, 8 * CAP), F32),
+            pltpu.VMEM((n_dev, 8 * CAP), F32),
             dma((n_blk,)),
             dma((3, 9)), dma((3, 9)), dma((3, 9)), dma((3, 9)),
             dma((3, n_row)), dma((3, n_row)), dma((3, n_col)), dma((3, n_col)),
@@ -548,7 +602,6 @@
         n_row, n_col, neighbours, right_side, anchor, owners.reshape(n_blk, side),
         row_offset.reshape(n_blk, side), col_offset.reshape(n_blk, side), tiles,
     )
-    arrived = arrived.reshape(n_row * n_col, 128)
     at_row = arrived[:, :CAP].reshape(-1)
     at_col = arrived[:, CAP:2 * CAP].reshape(-1)
     grid_rows, grid_cols = macro_density.shape

time: 148 us -> 135 us (0.912)
  Pallas kernels: 108 us -> 95.5 us
    pallas_call x1, Pallas kernels: 76.3 us -> 62.9 us  [solve(): pl.pallas_call(functools.partial(solve_kernel, n_row, n_col), name='solve...]
where the time goes in v2:
time: 135 us
  Pallas kernels  95.5 us (71%)
  matrix products  22 us (16%)
  local copies, waits for them, and re-layouts  15.2 us (11%)
  other arithmetic  1.39 us (1%)
    pallas_call x1, Pallas kernels, solve(): pl.pallas_call(functools.partial(solve_kernel, n_row, n_col), name='solve...  62.9 us
    dot_general x1, matrix products, per_device(): lax.dot_general(window_of(at_row, grid_rows), window_of(at_col, grid_cols...  22 us
    pallas_call x1, Pallas kernels, diffuse(): pl.pallas_call(functools.partial(diffuse_kernel, n_row, n_col), name='dif...  21.6 us
    pallas_call x1, Pallas kernels, exchange_edges(): pl.pallas_call(functools.partial(edge_kernel, n_row, n_col), name='grid_e...  11 us
    unnamed x19, local copies, waits for them, and re-layouts  10.7 us

profile of v2, /device:TPU:1, one launch (start us, length us, event | category | flops | bytes accessed | tf_op | source)
XLA Modules:
  0.0 134.8 jit_solution(1232256067803260103)
XLA Ops:
  0.6 0.8 copy.13.nbr_ref
  1.4 0.5 broadcast.91
  1.9 1.4 %reduce.3 = s32[2048]{0:T(1024)S(1)} reduce(s32[2048,1]{0,1:T(1,128)} %param.12, s32[]{:T(128)} %broadcast.91), dimensions={1}, to_apply=%param.12.reduce_sub_computation.3 | reduce | bytes 16388 | tf_op args[4]
  3.3 0.7 reshape.58.roff_ref
  4.0 0.7 reshape.59.coff_ref
  4.7 0.0 copy-start.4
  4.7 0.7 copy-done.4
  5.4 0.0 copy-start.7
  5.4 0.7 copy-done.7
  6.1 62.9 %solve_and_route.1 = (f32[8,2,256]{2,1,0:T(2,128)S(1)}, f32[128,128]{1,0:T(8,128)S(1)}) custom-call(s32[8,4]{1,0:T(8,128)S(1)} %copy.13.nbr_ref, f32[8,2,256]{2,1,0:T(2,128)S(1)} %copy-done.4, f32[8,256]{1,0:T(8,128)S(1)} %copy-done.7, s32[8,256]{1,0:T(8,128)S(1)} %reshape.57.owner_ref, s32[8,256]{1,0:T(8,128)S(1)} %reshape.58.roff_ref, ...), custom_call_target="tpu_custom_call" | custom-call | flops 1000000000 | bytes 8388608 | tf_op jit(solution)/shard_map/solve_and_route/pallas_call | solution.py:378
  69.0 0.1 fusion.25
  69.1 0.1 reshape.60
  69.2 0.1 reshape.61
  69.3 22.0 %fusion.17.field_ref = f32[2048,512]{1,0:T(8,128)S(1)} fusion(f32[2048,512]{1,0:T(8,128)} %param.15, f32[4096]{0:T(1024)S(1)} %reshape.61, f32[512]{0:T(512)S(1)} %iota_convert_fusion.1, s32[4096]{0:T(1024)S(1)} %get-tuple-element.23, s32[4096]{0:T(1024)S(1)} %get-tuple-element.22, f32[4096]{0:T(1024)S(1)} %reshape.60, f32[2048]{0:T(1024)S(1)} %iota_convert_fusion, ...), kind=kOutput, calls=%fused_computation.21 | convolution fusion | flops 8674869248 | bytes 8497152 | tf_op jit(solution)/shard_map/dot_general | solution.py:616
  91.3 0.6 fusion.24
  91.9 0.4 slice_bitcast_fusion
  92.3 0.0 copy-start
  92.3 2.0 %copy-done = f32[2048,512]{1,0:T(8,128)} copy-done((f32[2048,512]{1,0:T(8,128)}, f32[2048,512]{1,0:T(8,128)S(1)}, u32[]{:S(2)}) %copy-start) | copy-done | bytes 4194328
  94.3 0.9 copy.15.right_ref
  95.2 0.9 copy.14.left_ref
  96.1 11.0 %grid_edges.1 = (f32[8,512]{1,0:T(8,128)}, f32[8,512]{1,0:T(8,128)}, f32[8,2304]{1,0:T(8,128)}, f32[8,2304]{1,0:T(8,128)}) custom-call(f32[8,512]{1,0:T(8,128)} %get-tuple-element.17.top_ref, f32[8,512]{1,0:T(8,128)} %get-tuple-element.16.bottom_ref, f32[8,2048]{1,0:T(8,128)} %copy.14.left_ref, f32[8,2048]{1,0:T(8,128)} %copy.15.right_ref), custom_call_target="tpu_custom_call" | custom-call | tf_op jit(solution)/shard_map/grid_edges/pallas_call | solution.py:465
  107.2 0.0 copy-start.1
  107.2 2.2 %copy-done.1 = f32[2048,512]{1,0:T(8,128)S(1)} copy-done((f32[2048,512]{1,0:T(8,128)S(1)}, f32[2048,512]{1,0:T(8,128)}, u32[]{:S(2)}) %copy-start.1) | copy-done | bytes 4194328
  109.4 0.0 copy-start.2
  109.4 0.9 copy-done.2
  110.3 0.0 copy-start.3
  110.3 0.9 copy-done.3
  111.1 0.0 copy-start.5
  111.1 0.7 copy-done.5
  111.9 0.0 copy-start.6
  111.9 0.7 copy-done.6
  112.6 21.6 %diffuse.1 = f32[2048,512]{1,0:T(8,128)} custom-call(f32[2048,512]{1,0:T(8,128)S(1)} %copy-done.1, f32[8,512]{1,0:T(8,128)S(1)} %copy-done.5, f32[8,512]{1,0:T(8,128)S(1)} %copy-done.6, f32[8,2304]{1,0:T(8,128)S(1)} %copy-done.2, f32[8,2304]{1,0:T(8,128)S(1)} %copy-done.3), custom_call_target="tpu_custom_call" | custom-call | flops 20971520 | bytes 8388608 | tf_op jit(solution)/shard_map/diffuse/pallas_call | solution.py:581
  134.2 0.6 copy.17
  (4 shorter events, 0.0 us)
Async XLA Ops:
  4.7 0.7 copy-start.4
  5.4 0.7 copy-start.7
  92.3 2.0 %copy-start = (f32[2048,512]{1,0:T(8,128)}, f32[2048,512]{1,0:T(8,128)S(1)}, u32[]{:S(2)}) copy-start(f32[2048,512]{1,0:T(8,128)S(1)} %fusion.17.field_ref) | copy-start | bytes 12582916
  107.2 2.2 %copy-start.1 = (f32[2048,512]{1,0:T(8,128)S(1)}, f32[2048,512]{1,0:T(8,128)}, u32[]{:S(2)}) copy-start(f32[2048,512]{1,0:T(8,128)} %copy-done) | copy-start | bytes 12582916
  109.4 0.9 copy-start.2
  110.3 0.9 copy-start.3
  111.1 0.7 copy-start.5
  111.9 0.7 copy-start.6

commit v3 on v2

--- a/solution.py
+++ b/solution.py
@@ -416,183 +416,287 @@
     )(neighbours, right_side, anchor, owners, row_offset, col_offset, tiles)
 
 
-def edge_kernel(n_row, n_col, top_ref, bottom_ref, left_ref, right_ref, up_ref, down_ref, west_ref, east_ref, ss, rs):
+def grid_kernel(
+    n_row, n_col,
+    pos_ref, macro_ref, out_ref,
+    one, two, bell_col, left_sel, right_sel, low_part, high_part, place,
+    top_s, bottom_s, west_s, east_s, up_r, down_r, west_r, east_r, keep_top, keep_bottom, side,
+    in_sem, out_sem, ss, rs,
+):
+    length, width = macro_ref.shape
+    n_dev = n_row * n_col
+    n_slot = bell_col.shape[0]
+    n_chunk = length // CHUNK
     me_r = lax.axis_index("row")
     me_c = lax.axis_index("col")
-    barrier = pltpu.get_barrier_semaphore()
+    log2e = 1.4426950408889634
 
     def at(dr, dc):
         return lax.rem(me_r + dr + n_row, n_row), lax.rem(me_c + dc + n_col, n_col)
 
-    for g, (dr, dc) in enumerate(AROUND):
-        if g != 4:
-            row, col = at(dr, dc)
-            pl.semaphore_signal(barrier, inc=1, device_id={"row": row, "col": col}, device_id_type=MESH)
+    def load(i):
+        return pltpu.make_async_copy(
+            macro_ref.at[pl.ds(i * BAND, BAND)], one.at[pl.ds(8 + i * BAND, BAND)], in_sem.at[i]
+        )
+
+    def store(buf, i):
+        return pltpu.make_async_copy(
+            buf.at[pl.ds(8 + i * CHUNK, CHUNK)], out_ref.at[pl.ds(i * CHUNK, CHUNK)], out_sem.at[i]
+        )
+
+    barrier = pltpu.get_barrier_semaphore()
+    around = sorted((g for g in range(9) if g != 4), key=lambda g: -abs(AROUND[g][0]) - 2 * abs(AROUND[g][1]))
+    for g in around:
+        row, col = at(*AROUND[g])
+        pl.semaphore_signal(barrier, inc=1, device_id={"row": row, "col": col}, device_id_type=MESH)
+    for i in range(length // BAND):
+        load(i).start()
+    rim = jnp.zeros((8, width), F32)
+    for buf in (one, two):
+        buf[0:8, :] = rim
+        buf[length + 8:length + 16, :] = rim
+
+    turned = jnp.transpose(pos_ref[...])
+    at_row = turned[0:CAP]
+    start = jnp.clip(jnp.floor(at_row) - 7.0, 0.0, length - 16.0)
+    block = jnp.floor(start * (1.0 / 32.0))
+    rows48 = iota((48, n_dev), 0).astype(F32)
+    for j in range(CAP):
+        u = rows48 + 32.0 * block[j:j + 1]
+        d = u - at_row[j:j + 1]
+        inside = jnp.abs(u - (start[j:j + 1] + 7.5)) < 8.0
+        bell = jnp.where(inside, jnp.exp2(d * d * (-0.5 * log2e)), 0.0).astype(BF16)
+        here = slice(j * n_dev, (j + 1) * n_dev)
+        low_part[:, here] = bell[0:32]
+        high_part[:, here] = jnp.concatenate([bell[32:48], jnp.zeros((16, n_dev), BF16)], axis=0)
+        place[:, here] = jnp.broadcast_to(block[j:j + 1], (32, n_dev)).astype(BF16)
+
+    all_pos = pos_ref[...]
+    at_col = pltpu.roll(all_pos, 128 - CAP, 1)
+    middle = jnp.clip(jnp.floor(at_col) - 7.0, 0.0, width - 16.0) + 7.5
+    v = iota((1, width), 1).astype(F32)
+
+    def some_columns(i, carry):
+        p, m = carry
+        for k in range(4):
+            d = v - p[:, k:k + 1]
+            inside = jnp.abs(v - m[:, k:k + 1]) < 8.0
+            bell = jnp.where(inside, jnp.exp2(d * d * (-0.5 * log2e)), 0.0)
+            bell_col[pl.ds(pl.multiple_of((i * 4 + k) * n_dev, n_dev), n_dev), :] = bell.astype(BF16)
+        return pltpu.roll(p, 124, 1), pltpu.roll(m, 124, 1)
+
+    lax.fori_loop(0, CAP // 4, some_columns, (at_col, middle))
+
+    def build(dst, band):
+        for sub in range(BAND // 32):
+            block_id = (band * (BAND // 32) + sub).astype(F32)
+            first = place[...] == jnp.full((32, n_slot), block_id, F32).astype(BF16)
+            second = place[...] == jnp.full((32, n_slot), block_id - 1.0, F32).astype(BF16)
+            zero = jnp.zeros((32, n_slot), BF16)
+            dst[sub * 32:(sub + 1) * 32, :] = jnp.where(
+                first, low_part[...], jnp.where(second, high_part[...], zero)
+            )
+
+    def product(src, band):
+        load(band).wait()
+        here = pl.ds(pl.multiple_of(8 + band * BAND, 8), BAND)
+        one[here, :] = one[here, :] + nn_dot(src[...], bell_col[...])
+
+    build(left_sel, jnp.int32(0))
+
+    def two_bands(i, carry):
+        build(right_sel, 2 * i + 1)
+        product(left_sel, 2 * i)
+        build(left_sel, jnp.minimum(2 * i + 2, length // BAND - 1))
+        product(right_sel, 2 * i + 1)
+        return carry
+
+    lax.fori_loop(0, length // BAND // 2, two_bands, 0)
+
+    top_s[...] = one[8:16, :]
+    bottom_s[...] = one[length:length + 8, :]
+    keep_top[...] = one[8:24, :]
+    keep_bottom[...] = one[length - 8:length + 8, :]
+    lane = iota((1, 128), 1)
+    for i in range(length // 128):
+        here = slice(8 + i * 128, 8 + (i + 1) * 128)
+        tile = jnp.transpose(jnp.where(lane < 64, one[here, 0:128], one[here, width - 128:width]))
+        west_s[:, i * 128:(i + 1) * 128] = tile[0:8]
+        east_s[:, i * 128:(i + 1) * 128] = tile[120:128]
+
     pl.semaphore_wait(barrier, 8)
-    length = left_ref.shape[1]
     first = (slice(None), pl.ds(0, 128))
     last = (slice(None), pl.ds(length - 128, 128))
     inner = (slice(None), pl.ds(128, length))
     above = (slice(None), pl.ds(0, 128))
     below = (slice(None), pl.ds(length + 128, 128))
     plan = {
-        (-1, 0): (top_ref, down_ref),
-        (1, 0): (bottom_ref, up_ref),
-        (0, -1): (left_ref, east_ref.at[inner]),
-        (0, 1): (right_ref, west_ref.at[inner]),
-        (-1, -1): (left_ref.at[first], east_ref.at[below]),
-        (-1, 1): (right_ref.at[first], west_ref.at[below]),
-        (1, -1): (left_ref.at[last], east_ref.at[above]),
-        (1, 1): (right_ref.at[last], west_ref.at[above]),
+        (-1, 0): (top_s, down_r),
+        (1, 0): (bottom_s, up_r),
+        (0, -1): (west_s, east_r.at[inner]),
+        (0, 1): (east_s, west_r.at[inner]),
+        (-1, -1): (west_s.at[first], east_r.at[below]),
+        (-1, 1): (east_s.at[first], west_r.at[below]),
+        (1, -1): (west_s.at[last], east_r.at[above]),
+        (1, 1): (east_s.at[last], west_r.at[above]),
     }
     copies = []
-    for g, side in enumerate(AROUND):
-        if g != 4:
-            src, dst = plan[side]
-            row, col = at(*side)
-            copy = remote(src, dst, ss.at[g], rs.at[g], row, col)
-            copy.start()
-            copies.append(copy)
+    for g in around:
+        src, dst = plan[AROUND[g]]
+        row, col = at(*AROUND[g])
+        copy = remote(src, dst, ss.at[g], rs.at[g], row, col)
+        copy.start()
+        copies.append(copy)
+
+    def summed(src, begin, n):
+        window = src[pl.ds(pl.multiple_of(begin - 8, 8), n + 16), :]
+        centre = window[8:8 + n]
+        return (
+            (centre + window[7:7 + n]) + (window[9:9 + n] + pltpu.roll(centre, 1, 1)) + pltpu.roll(centre, width - 1, 1)
+        )
+
+    for src, dst in ((one, two), (two, one), (one, two)):
+
+        def strip(i, carry, src=src, dst=dst):
+            begin = pl.multiple_of(8 + i * CHUNK, 8)
+            dst[pl.ds(begin, CHUNK), :] = summed(src, begin, CHUNK)
+            return carry
+
+        lax.fori_loop(0, n_chunk, strip, 0)
+
     for copy in copies:
         copy.wait_recv()
-    for copy in copies:
-        copy.wait_send()
-
-
-def exchange_edges(n_row, n_col, top, bottom, left, right):
-    vmem = pl.BlockSpec(memory_space=pltpu.VMEM)
-    length, width = left.shape[1], top.shape[1]
-    return pl.pallas_call(
-        functools.partial(edge_kernel, n_row, n_col),
-        name="grid_edges",
-        out_shape=(
-            jax.ShapeDtypeStruct((8, width), F32),
-            jax.ShapeDtypeStruct((8, width), F32),
-            jax.ShapeDtypeStruct((8, length + 256), F32),
-            jax.ShapeDtypeStruct((8, length + 256), F32),
-        ),
-        in_specs=[vmem] * 4,
-        out_specs=(vmem,) * 4,
-        scratch_shapes=[pltpu.SemaphoreType.DMA((9,)), pltpu.SemaphoreType.DMA((9,))],
-        compiler_params=pltpu.CompilerParams(collective_id=1, has_side_effects=True),
-    )(top, bottom, left, right)
-
-
-CHUNK = 128
-STRIP = 64
-
-
-def diffuse_kernel(n_row, n_col, field_ref, up_ref, down_ref, west_ref, east_ref, out_ref, one, two, in_sem, out_sem):
-    length, width = field_ref.shape
-    wide = width + 128
-    n_chunk = length // CHUNK
-    me_r = lax.axis_index("row")
-    me_c = lax.axis_index("col")
-
-    def load(i):
-        return pltpu.make_async_copy(
-            field_ref.at[pl.ds(i * CHUNK, CHUNK)], one.at[pl.ds(8 + i * CHUNK, CHUNK), pl.ds(0, width)], in_sem.at[i]
-        )
-
-    for i in range(n_chunk):
-        load(i).start()
     not_first_row = (me_r > 0).astype(F32)
     not_last_row = (me_r < n_row - 1).astype(F32)
     not_first_col = (me_c > 0).astype(F32)
     not_last_col = (me_c < n_col - 1).astype(F32)
-    lane = iota((1, 128), 1)
-    keep_lane = jnp.where(lane < 8, not_last_col, jnp.where(lane >= 120, not_first_col, 0.0))
-    one[0:8, 0:width] = up_ref[...] * not_first_row
-    one[length + 8:length + 16, 0:width] = down_ref[...] * not_last_row
-    gap = jnp.zeros((112, 128), F32)
-    for i in range(length // 128 + 2):
-        here = pl.ds(i * 128, 128)
-        tile = jnp.transpose(jnp.concatenate([east_ref[:, here], gap, west_ref[:, here]], axis=0)) * keep_lane
-        if i == 0:
-            one[0:8, width:wide] = tile[120:128] * not_first_row
-        elif i == length // 128 + 1:
-            one[length + 8:length + 16, width:wide] = tile[0:8] * not_last_row
-        else:
-            one[8 + (i - 1) * 128:8 + i * 128, width:wide] = tile
-    for i in range(n_chunk):
-        load(i).wait()
-
-    keep_cols = jnp.concatenate([jnp.ones((1, width), F32), keep_lane], axis=1)
-
-    def summed(src, start, n):
-        window = src[pl.ds(pl.multiple_of(start - 8, 8), n + 16), :]
-        centre = window[8:8 + n]
-        above = window[7:7 + n]
-        below = window[9:9 + n]
-        return (centre + above) + (below + pltpu.roll(centre, 1, 1)) + pltpu.roll(centre, wide - 1, 1)
-
-    def edge(src, dst):
-        for start, keep in ((0, not_first_row), (length + 8, not_last_row)):
-            c = src[start:start + 8, :]
-            if start == 0:
-                above = pltpu.roll(c, 1, 0)
-                below = src[1:9, :]
-            else:
-                above = src[start - 1:start + 7, :]
-                below = pltpu.roll(c, 7, 0)
-            total = c + above + below + pltpu.roll(c, 1, 1) + pltpu.roll(c, wide - 1, 1)
-            dst[start:start + 8, :] = total * keep_cols * keep
-
-    src, dst = one, two
+    scale = 0.2 ** STEPS
+
+    def cross(t):
+        n, m = t.shape
+        return (t + pltpu.roll(t, 1, 0)) + (pltpu.roll(t, n - 1, 0) + pltpu.roll(t, 1, 1)) + pltpu.roll(t, m - 1, 1)
+
+    pad = jnp.zeros((120, 128), F32)
+    corners = []
+    for halo, order in ((up_r, 0), (down_r, 1)):
+        for part in (halo[:, 0:128], halo[:, width - 128:width]):
+            corners.append(jnp.transpose(jnp.concatenate([pad, part] if order == 0 else [part, pad], axis=0)))
+    own_west = jnp.concatenate([corners[0][0:8], west_s[...], corners[2][0:8]], axis=1)
+    own_east = jnp.concatenate([corners[1][120:128], east_s[...], corners[3][120:128]], axis=1)
+    t = jnp.concatenate([west_r[...], own_west, own_east, east_r[...]], axis=0)
+    down32 = iota((32, 1), 0)
+    along = iota((1, length + 256), 1)
+    mask = jnp.where(down32 < 8, not_first_col, jnp.where(down32 >= 24, not_last_col, 1.0)) * jnp.where(
+        along < 128, jnp.where(along >= 120, not_first_row, 0.0),
+        jnp.where(along >= length + 128, jnp.where(along < length + 136, not_last_row, 0.0), 1.0),
+    )
+    t = t * mask
     for step in range(STEPS):
+        t = cross(t)
         if step < STEPS - 1:
-            edge(src, dst)
-
-            def strip(i, carry, src=src, dst=dst):
-                start = pl.multiple_of(8 + i * STRIP, 8)
-                total = summed(src, start, STRIP)
-                dst[pl.ds(start, STRIP), 0:width] = total[:, 0:width]
-                dst[pl.ds(start, STRIP), width:wide] = total[:, width:wide] * keep_lane
-                return carry
-
-            lax.fori_loop(0, length // STRIP, strip, 0)
-        else:
-
-            def strip(i, carry, src=src, dst=dst):
-                start = pl.multiple_of(8 + i * STRIP, 8)
-                total = summed(src, start, STRIP)
-                dst[pl.ds(start, STRIP), 0:width] = total[:, 0:width] * (0.2 ** STEPS)
-                return carry
-
-            for i in range(n_chunk):
-                lax.fori_loop(i * (CHUNK // STRIP), (i + 1) * (CHUNK // STRIP), strip, 0)
-                store_chunk(dst, out_ref, out_sem, i, width).start()
-        src, dst = dst, src
-    for i in range(n_chunk):
-        store_chunk(src, out_ref, out_sem, i, width).wait()
-
-
-def store_chunk(buf, out_ref, out_sem, i, width):
-    return pltpu.make_async_copy(
-        buf.at[pl.ds(8 + i * CHUNK, CHUNK), pl.ds(0, width)], out_ref.at[pl.ds(i * CHUNK, CHUNK)], out_sem.at[i]
-    )
-
-
-def diffuse(n_row, n_col, field, up, down, west, east):
-    length, width = field.shape
-    vmem = pl.BlockSpec(memory_space=pltpu.VMEM)
-    hbm = pl.BlockSpec(memory_space=pl.ANY)
-    n_chunk = length // CHUNK
+            t = t * mask
+    side[...] = t * scale
+
+    def rim_rows(halo, kept, keep, at_top):
+        r = jnp.concatenate([halo * keep, kept] if at_top else [kept, halo * keep], axis=0)
+        near = iota((24, 1), 0)
+        flag = jnp.where((near < 8) if at_top else (near >= 16), keep, 1.0)
+        for step in range(STEPS):
+            r = cross(r)
+            if step < STEPS - 1:
+                r = r * flag
+        return (r[8:16] if at_top else r[8:16]) * scale
+
+    zero112 = jnp.zeros((112, 128), F32)
+
+    def side_tile(i):
+        here = pl.ds(pl.multiple_of((i + 1) * 128, 128), 128)
+        return jnp.transpose(jnp.concatenate([side[8:16, here], zero112, side[16:24, here]], axis=0))
+
+    def finish(i, carry):
+        begin = pl.multiple_of(8 + i * CHUNK, 8)
+        total = summed(two, begin, CHUNK) * scale
+        for h in range(CHUNK // 128):
+            rows_h = slice(h * 128, (h + 1) * 128)
+            tile = side_tile(i * (CHUNK // 128) + h)
+            here = pl.ds(pl.multiple_of(begin + h * 128, 8), 128)
+            one[here, 0:128] = jnp.where(lane < 4, tile, total[rows_h, 0:128])
+            one[here, 128:width - 128] = total[rows_h, 128:width - 128]
+            one[here, width - 128:width] = jnp.where(lane >= 124, tile, total[rows_h, width - 128:width])
+        return carry
+
+    def start_store(i, carry):
+        finish(i, carry)
+        store(one, i).start()
+        return carry
+
+    lax.fori_loop(1, n_chunk - 1, start_store, 0)
+    for i, at_row8, rim8 in (
+        (0, 8, rim_rows(up_r[...], keep_top[...], not_first_row, True)),
+        (n_chunk - 1, length, rim_rows(down_r[...], keep_bottom[...], not_last_row, False)),
+    ):
+        finish(jnp.int32(i), 0)
+        one[at_row8:at_row8 + 8, 0:128] = jnp.where(lane < 4, one[at_row8:at_row8 + 8, 0:128], rim8[:, 0:128])
+        one[at_row8:at_row8 + 8, 128:width - 128] = rim8[:, 128:width - 128]
+        one[at_row8:at_row8 + 8, width - 128:width] = jnp.where(
+            lane >= 124, one[at_row8:at_row8 + 8, width - 128:width], rim8[:, width - 128:width]
+        )
+        store(one, i).start()
+
+    def finish_store(i, carry):
+        store(one, i).wait()
+        return carry
+
+    lax.fori_loop(0, n_chunk, finish_store, 0)
+    for copy in copies:
+        copy.wait_send()
+
+
+CHUNK = 128
+BAND = 256
+
+
+def spread_and_diffuse(n_row, n_col, positions, macro):
+    length, width = macro.shape
+    n_slot = n_row * n_col * CAP
+    any_space = pl.BlockSpec(memory_space=pl.ANY)
+    dma = pltpu.SemaphoreType.DMA
     return pl.pallas_call(
-        functools.partial(diffuse_kernel, n_row, n_col),
-        name="diffuse",
-        out_shape=jax.ShapeDtypeStruct(field.shape, F32),
-        in_specs=[hbm] + [vmem] * 4,
-        out_specs=hbm,
+        functools.partial(grid_kernel, n_row, n_col),
+        name="spread_and_diffuse",
+        out_shape=jax.ShapeDtypeStruct(macro.shape, F32),
+        in_specs=[pl.BlockSpec(memory_space=pltpu.VMEM), any_space],
+        out_specs=any_space,
         scratch_shapes=[
-            pltpu.VMEM((length + 16, width + 128), F32),
-            pltpu.VMEM((length + 16, width + 128), F32),
-            pltpu.SemaphoreType.DMA((n_chunk,)),
-            pltpu.SemaphoreType.DMA((n_chunk,)),
+            pltpu.VMEM((length + 16, width), F32),
+            pltpu.VMEM((length + 16, width), F32),
+            pltpu.VMEM((n_slot, width), BF16),
+            pltpu.VMEM((BAND, n_slot), BF16),
+            pltpu.VMEM((BAND, n_slot), BF16),
+            pltpu.VMEM((32, n_slot), BF16),
+            pltpu.VMEM((32, n_slot), BF16),
+            pltpu.VMEM((32, n_slot), BF16),
+            pltpu.VMEM((8, width), F32),
+            pltpu.VMEM((8, width), F32),
+            pltpu.VMEM((8, length), F32),
+            pltpu.VMEM((8, length), F32),
+            pltpu.VMEM((8, width), F32),
+            pltpu.VMEM((8, width), F32),
+            pltpu.VMEM((8, length + 256), F32),
+            pltpu.VMEM((8, length + 256), F32),
+            pltpu.VMEM((16, width), F32),
+            pltpu.VMEM((16, width), F32),
+            pltpu.VMEM((32, length + 256), F32),
+            dma((length // BAND,)),
+            dma((length // CHUNK,)),
+            dma((9,)),
+            dma((9,)),
         ],
-        compiler_params=pltpu.CompilerParams(vmem_limit_bytes=32 * 2**20),
-        cost_estimate=pl.CostEstimate(flops=4 * 5 * length * width, bytes_accessed=8 * length * width, transcendentals=0),
-    )(field, up, down, west, east)
+        compiler_params=pltpu.CompilerParams(
+            collective_id=1, has_side_effects=True, vmem_limit_bytes=48 * 2**20
+        ),
+        cost_estimate=pl.CostEstimate(flops=10**10, bytes_accessed=8 * length * width, transcendentals=0),
+    )(positions, macro)
 
 
 def per_device(right_side, anchor, tiles, neighbours, owners, row_offset, col_offset, macro_density):
@@ -602,25 +706,7 @@
         n_row, n_col, neighbours, right_side, anchor, owners.reshape(n_blk, side),
         row_offset.reshape(n_blk, side), col_offset.reshape(n_blk, side), tiles,
     )
-    at_row = arrived[:, :CAP].reshape(-1)
-    at_col = arrived[:, CAP:2 * CAP].reshape(-1)
-    grid_rows, grid_cols = macro_density.shape
-
-    def window_of(position, limit):
-        start_cell = jnp.clip(jnp.floor(position).astype(jnp.int32) - 7, 0, limit - 16)
-        cells = lax.iota(jnp.int32, limit)[None, :]
-        inside = ((cells >= start_cell[:, None]) & (cells < start_cell[:, None] + 16)).astype(F32)
-        offset = cells.astype(F32) - position[:, None]
-        return (jnp.exp(-0.5 * offset * offset) * inside).astype(BF16)
-
-    spread = lax.dot_general(
-        window_of(at_row, grid_rows), window_of(at_col, grid_cols), (((0,), (0,)), ((), ())), preferred_element_type=F32
-    )
-    field = macro_density + spread
-    edges = exchange_edges(
-        n_row, n_col, field[:8], field[-8:], field[:, :8].T, field[:, -8:].T
-    )
-    return solution, diffuse(n_row, n_col, field, *edges)
+    return solution, spread_and_diffuse(n_row, n_col, arrived, macro_density)
 
 
 def solution(mesh):

time: 135 us -> 106 us (0.79)
  matrix products: 22 us -> 0 us
  local copies, waits for them, and re-layouts: 15.2 us -> 6.71 us
    dot_general x1 -> x0, matrix products: 22 us -> none  [per_device(): lax.dot_general(window_of(at_row, grid_rows), window_of(at_col, grid_cols...]
    unnamed x19 -> x8, local copies, waits for them, and re-layouts: 10.7 us -> 5.3 us
    transpose x3 -> x0, local copies, waits for them, and re-layouts: 2.22 us -> none  [the longest x2 1.29 us: per_device(): field[:, -8:]]
    pallas_call x2 -> x1, Pallas kernels: 32.6 us -> 33.5 us  [spread_and_diffuse(): pl.pallas_call(functools.partial(grid_kernel, n_row, n_col), name='spread...]
where the time goes in v3:
time: 106 us; the launch traced here: 105 us
  Pallas kernels  96.3 us (91%)
  local copies, waits for them, and re-layouts  6.71 us (6%)
  other arithmetic  1.36 us (1%)
    pallas_call x1, Pallas kernels, solve(): pl.pallas_call(functools.partial(solve_kernel, n_row, n_col), name='solve...  62.8 us
    pallas_call x1, Pallas kernels, spread_and_diffuse(): pl.pallas_call(functools.partial(grid_kernel, n_row, n_col), name='spread...  33.5 us
    unnamed x8, local copies, waits for them, and re-layouts  5.3 us

profile of v3, /device:TPU:1, one launch (start us, length us, event | category | flops | bytes accessed | tf_op | source)
XLA Modules:
  0.0 105.0 jit_solution(10978050745534774657)
XLA Ops:
  0.6 0.8 copy.10.nbr_ref
  1.4 0.5 broadcast.3
  1.9 1.4 %reduce.3 = s32[2048]{0:T(1024)S(1)} reduce(s32[2048,1]{0,1:T(1,128)} %param.12, s32[]{:T(128)} %broadcast.3), dimensions={1}, to_apply=%param.12.reduce_sub_computation.3 | reduce | bytes 16388 | tf_op args[4]
  3.3 0.7 reshape.14.roff_ref
  4.0 0.7 reshape.15.coff_ref
  4.7 0.0 copy-start
  4.7 0.7 copy-done
  5.4 0.0 copy-start.1
  5.4 0.7 copy-done.1
  6.1 62.8 %solve_and_route.1 = (f32[8,2,256]{2,1,0:T(2,128)S(1)}, f32[128,128]{1,0:T(8,128)S(1)}) custom-call(s32[8,4]{1,0:T(8,128)S(1)} %copy.10.nbr_ref, f32[8,2,256]{2,1,0:T(2,128)S(1)} %copy-done, f32[8,256]{1,0:T(8,128)S(1)} %copy-done.1, s32[8,256]{1,0:T(8,128)S(1)} %reshape.13.owner_ref, s32[8,256]{1,0:T(8,128)S(1)} %reshape.14.roff_ref, ...), custom_call_target="tpu_custom_call" | custom-call | flops 1000000000 | bytes 8388608 | tf_op jit(solution)/shard_map/solve_and_route/pallas_call | solution.py:378
  68.9 33.5 %spread_and_diffuse.1 = f32[2048,512]{1,0:T(8,128)S(1)} custom-call(f32[128,128]{1,0:T(8,128)S(1)} %get-tuple-element.5.pos_ref, f32[2048,512]{1,0:T(8,128)} %macro_ref.1), custom_call_target="tpu_custom_call" | custom-call | flops 10000000000 | bytes 8388608 | tf_op jit(solution)/shard_map/spread_and_diffuse/pallas_call | solution.py:664
  102.4 0.6 copy.13
  103.0 2.0 %copy.14 = f32[2048,512]{1,0:T(8,128)} copy(f32[2048,512]{1,0:T(8,128)S(1)} %spread_and_diffuse.1) | data formatting | bytes 8388608
  (1 shorter events, 0.0 us)
Async XLA Ops:
  4.7 0.7 copy-start
  5.4 0.7 copy-start.1

commit v4 on v3

--- a/solution.py
+++ b/solution.py
@@ -45,10 +45,11 @@
 
 def solve_kernel(
     n_row, n_col,
-    nbr_ref, rhs_ref, anchor_ref, owner_ref, roff_ref, coff_ref, tiles_ref,
+    nbr_hbm, rhs_hbm, anchor_hbm, owner_hbm, roff_hbm, coff_hbm, tiles_ref,
     sol_ref, pos_ref,
     stage, thi, tlo, xbuf, sel, spread_sel, gath, terms, back, recv,
     ar_row, ar_col, own_hot, rank_sc, weight_sc, out_rows, mid_rows, end_rows, table_sc,
+    own_sel, own_g, down_sc, sums_sc, far_sum, down_sum, nbr_sc, rhs_ref, anchor_ref, owner_ref, roff_ref, coff_ref, small_sem,
     tile_sem, fs, fr, bs, br, rs, rr, cs, cr, away1, got, away2, land, keep_sem,
 ):
     n_blk, fan, side, _ = thi.shape
@@ -62,6 +63,15 @@
     col_order = sorted(range(1, n_col), key=lambda d: -(min(d // 4, 4 - d // 4) + min(d % 4, 4 - d % 4)))
     around = sorted((g for g in range(9) if g != 4), key=lambda g: -abs(AROUND[g][0]) - 2 * abs(AROUND[g][1]))
 
+    small = [
+        pltpu.make_async_copy(src, dst, small_sem.at[i])
+        for i, (src, dst) in enumerate((
+            (rhs_hbm, rhs_ref), (owner_hbm, owner_ref), (nbr_hbm, nbr_sc),
+            (anchor_hbm, anchor_ref), (roff_hbm, roff_ref), (coff_hbm, coff_ref),
+        ))
+    ]
+    for copy in small:
+        copy.start()
     for b in range(n_blk):
         pltpu.make_async_copy(tiles_ref.at[b], stage.at[b], tile_sem.at[b]).start()
 
@@ -79,6 +89,8 @@
     below = iota((side - 9 * rows, side), 0)
     for it in range(3):
         xbuf[it, 9 * rows:side, :] = jnp.where(below == 0, 1.0, 0.0)
+    for copy in small[:2]:
+        copy.wait()
     for b in range(n_blk):
         xbuf[0, own_lo + 2 * b:own_lo + 2 * b + 2, :] = rhs_ref[b]
 
@@ -86,7 +98,7 @@
     count = jnp.zeros((n_dev, 1), F32)
     held = jnp.zeros((1, n_dev), F32)
     for b in range(n_blk):
-        hot = (owner_ref[b:b + 1, :] == iota((n_dev, side), 0)).astype(F32)
+        hot = (owner_ref[0:1, b * side:(b + 1) * side] == iota((n_dev, side), 0)).astype(F32)
         before = nn_dot(hot.astype(BF16), upper) + count
         rank_sc[b:b + 1, :] = jnp.sum(hot * before, axis=0, keepdims=True)
         count = count + jnp.sum(hot, axis=1, keepdims=True)
@@ -139,16 +151,24 @@
     )
     moves = (part_row < 6).astype(jnp.int32)
 
+    lane_own = iota((8, 4 * rows), 1)
+    own_col = jnp.where(
+        part_row < 6, (part_row // 2) * rows + lax.rem(part_row, 2), jnp.where(part_row == 6, 3 * rows, -1)
+    )
+
     def select_row(q, slot):
         sel[q:q + 8, :] = (lane3 == base_col + moves * (2 * slot)).astype(F32).astype(BF16)
 
+    for copy in small[2:]:
+        copy.wait()
     for b in range(n_blk):
         for k in range(fan):
-            named = nbr_ref[b, k]
+            named = nbr_sc[k, b]
             dev = named // n_blk
             slot = ((dev // n_col - me_r + 1) * 3 + (lax.rem(dev, n_col) - me_c + 1)) * n_blk + lax.rem(named, n_blk)
             select_row((b * fan + k) * 8, slot)
         select_row(q_own + b * 8, 4 * n_blk + b)
+        own_sel[b * 8:(b + 1) * 8, :] = (lane_own == own_col + moves * (2 * b)).astype(F32).astype(BF16)
     sel_t = sel[:, 0:side].astype(F32) + sel[:, side:2 * side].astype(F32) + sel[:, 2 * side:].astype(F32)
     spread_sel[...] = jnp.transpose(jnp.concatenate([sel_t, jnp.zeros((384 - q_all, side), F32)], axis=0)).astype(BF16)
     terms[...] = jnp.zeros_like(terms)
@@ -164,35 +184,60 @@
 
     lax.fori_loop(0, n_blk, split_block, 0)
 
+    first_row = jnp.where(iota((rows, side), 0) == 0, 1.0, 0.0).astype(BF16)
+
+    def grouped(c, v):
+        return (v.reshape(q_own // 8, 8, side) * c[None]).reshape(q_own, side)
+
+    def over_parts(v):
+        return v + pltpu.roll(v, q_own - 2, 0) + pltpu.roll(v, q_own - 4, 0)
+
+    def own_products(it, own):
+        own_g[...] = nn_dot(own_sel[...], jnp.concatenate(split3(own) + (first_row,), axis=0))
+
+        def one_block(b, carry):
+            own_b = own_g[pl.ds(pl.multiple_of(b * 8, 8), 8), :].astype(BF16)
+            for k in range(fan):
+                q = pl.multiple_of((b * fan + k) * 8, 8)
+                down = nn_dot(own_b, thi[b, k]) + nn_dot(own_b, tlo[b, k])
+                down_sc[pl.ds(q, 8), :] = down
+                if it == 0:
+                    sums_sc[pl.ds(q, 8), :] = jnp.broadcast_to(down[6:7, :], (8, side))
+            return carry
+
+        lax.fori_loop(0, n_blk, one_block, 0, unroll=2)
+        down_sum[it] = over_parts(down_sc[...])
+
+    def gather_far(it):
+        parts = jnp.concatenate(split3(xbuf[it]), axis=0)
+        gath[...] = nn_dot(sel[0:q_own, :], parts)
+
     def apply(it, after_forward=None):
         forward_wait(it)
         if after_forward is not None:
             after_forward()
-        parts = jnp.concatenate(split3(xbuf[it]), axis=0)
-        gath[...] = nn_dot(sel[...], parts)
+        gather_far(it)
 
         def one_block(b, carry):
-            own = gath[pl.ds(pl.multiple_of(q_own + b * 8, 8), 8), :]
-            own_b = own.astype(BF16)
             total = jnp.zeros((8, side), F32)
             for k in range(fan):
                 q = pl.multiple_of((b * fan + k) * 8, 8)
-                far = gath[pl.ds(q, 8), :]
-                far_b = far.astype(BF16)
+                far_b = gath[pl.ds(q, 8), :].astype(BF16)
                 total = total + nt_dot(far_b, thi[b, k]) + nt_dot(far_b, tlo[b, k])
-                down = nn_dot(own_b, thi[b, k]) + nn_dot(own_b, tlo[b, k])
-                terms[pl.ds(q, 8), :] = down[6:7, :] * far - down
             weight = total[6:7, :] + anchor_ref[pl.ds(b, 1), :]
             if it == 0:
                 weight_sc[pl.ds(b, 1), :] = weight
+            own = own_g[pl.ds(pl.multiple_of(b * 8, 8), 8), :]
             terms[pl.ds(pl.multiple_of(q_own + b * 8, 8), 8), :] = weight * own - total
             return carry
 
-        lax.fori_loop(0, n_blk, one_block, 0)
+        lax.fori_loop(0, n_blk, one_block, 0, unroll=2)
+        terms[0:q_own, :] = sums_sc[...] * gath[...] - down_sc[...]
         hi, mid, low = split3(terms[...])
         where_to = spread_sel[0:9 * rows, :]
         back[it] = nn_dot(where_to, hi) + nn_dot(where_to, mid) + nn_dot(where_to, low)
         backward(it)
+        far_sum[it] = over_parts(gath[...])
 
     def applied(it):
         backward_wait(it)
@@ -245,31 +290,46 @@
     def times(c, v):
         return jnp.concatenate([c] * (v.shape[0] // 8), axis=0) * v
 
+    rank_of = iota((CAP, side), 0)
+
+    def by_owner(values_of):
+        total = None
+        for b in range(n_blk):
+            mine = rank_of == rank_sc[b:b + 1, :].astype(jnp.int32)
+            placed = jnp.concatenate([jnp.where(mine, v, 0.0) for v in values_of(b)], axis=0)
+            for part in split3(placed):
+                more = nn_dot(part, own_hot[b])
+                total = more if total is None else total + more
+        return total
+
+    def both(v):
+        return lambda b: [v[2 * b:2 * b + 1, :], v[2 * b + 1:2 * b + 2, :]]
+
+    def offsets(b):
+        return [r[b * side:(b + 1) * side].reshape(1, side).astype(F32) for r in (roff_ref, coff_ref)]
+
     r0 = xbuf[0, own_lo:own_lo + rows, :]
+    own_products(0, r0)
     apply(0)
+    table_r0 = by_owner(both(r0))
+    table_off = by_owner(offsets)
     w0 = applied(0)
     xbuf[1, own_lo:own_lo + rows, :] = w0
     forward(1)
     dots_start(0, [(r0, r0), (r0, w0)])
+    own_products(1, w0)
     apply(1, lambda: dots_middle(0))
+    table_w0 = by_owner(both(w0))
     gamma0, curve0 = dots_end(0, 2)
     alpha0 = gamma0 / curve0
     z0 = applied(1)
     w1 = w0 - times(alpha0, z0)
     xbuf[2, own_lo:own_lo + rows, :] = w1
-    forward(2)
     r1 = r0 - times(alpha0, w0)
     dots_start(1, [(r1, r1), (r1, w1), (r1, w0)])
-
-    rank_of = iota((CAP, side), 0)
-    table = jnp.zeros((8 * CAP, n_dev), F32)
-    for b in range(n_blk):
-        mine = rank_of == rank_sc[b:b + 1, :].astype(jnp.int32)
-        values = [v[2 * b + c:2 * b + c + 1, :] for v in (r0, w0, w1) for c in (0, 1)]
-        values += [roff_ref[b:b + 1, :].astype(F32), coff_ref[b:b + 1, :].astype(F32)]
-        placed = jnp.concatenate([jnp.where(mine, v, 0.0) for v in values], axis=0)
-        for part in split3(placed):
-            table = table + nn_dot(part, own_hot[b])
+    forward(2)
+
+    table = jnp.concatenate([table_r0, table_w0, by_owner(both(w1)), table_off], axis=0)
     empty = iota((CAP, n_dev), 0).astype(F32) >= held
     table = jnp.concatenate(
         [table[0:6 * CAP], jnp.where(empty, NONE, table[6 * CAP:7 * CAP]), table[7 * CAP:]], axis=0
@@ -299,7 +359,12 @@
         copy.start()
         pending.append(copy)
 
+    own_products(2, w1)
     forward_wait(2)
+    gather_far(2)
+    far_r1 = far_sum[0] - grouped(alpha0, far_sum[1])
+    down_r1 = down_sum[0] - grouped(alpha0, down_sum[1])
+    far_w1 = over_parts(gath[...])
     gamma1, r1w1, r1w0 = dots_end(1, 3)
     beta0 = gamma1 / gamma0
     curve1 = r1w1 + 2.0 * beta0 * r1w0 + beta0 * beta0 * curve0
@@ -308,26 +373,9 @@
     s1 = w1 + times(beta0, w0)
     r2 = r1 - times(alpha1, s1)
 
-    near_w0 = xbuf[1, 0:9 * rows, :]
-    near_r1 = xbuf[0, 0:9 * rows, :] - times(alpha0, near_w0)
-    near_r2 = near_r1 - times(alpha1, xbuf[2, 0:9 * rows, :] + times(beta0, near_w0))
-    near_r2 = jnp.concatenate([near_r2, jnp.where(below == 0, 1.0, 0.0)], axis=0)
-    gath[...] = nn_dot(sel[...], jnp.concatenate(split3(near_r2), axis=0))
-
-    def energy_block(b, carry):
-        own_b = gath[pl.ds(pl.multiple_of(q_own + b * 8, 8), 8), :].astype(BF16)
-        for k in range(fan):
-            q = pl.multiple_of((b * fan + k) * 8, 8)
-            down = nn_dot(own_b, thi[b, k]) + nn_dot(own_b, tlo[b, k])
-            terms[pl.ds(q, 8), :] = down[6:7, :] * gath[pl.ds(q, 8), :] - 2.0 * down
-        return carry
-
-    lax.fori_loop(0, n_blk, energy_block, 0)
-
-    def over_parts(v):
-        return v + pltpu.roll(v, q_own - 2, 0) + pltpu.roll(v, q_own - 4, 0)
-
-    cross = over_parts(terms[0:q_own, :]) * over_parts(gath[0:q_own, :])
+    far_r2 = far_r1 - grouped(alpha1, far_w1 + grouped(beta0, far_sum[1]))
+    down_r2 = down_r1 - grouped(alpha1, down_sum[2] + grouped(beta0, down_sum[1]))
+    cross = far_r2 * (sums_sc[...] * far_r2 - 2.0 * down_r2)
     cross = jnp.sum(cross.reshape(q_own // 8, 8, side), axis=0)
     cross = jnp.where(iota((8, side), 0) < 2, cross, 0.0)
     weights = weight_sc[...]
@@ -382,7 +430,7 @@
             jax.ShapeDtypeStruct(right_side.shape, F32),
             jax.ShapeDtypeStruct((n_dev, 128), F32),
         ),
-        in_specs=[pl.BlockSpec(memory_space=pltpu.SMEM)] + [vmem] * 5 + [pl.BlockSpec(memory_space=pl.ANY)],
+        in_specs=[pl.BlockSpec(memory_space=pltpu.HBM)] * 7,
         out_specs=(vmem, vmem),
         scratch_shapes=[
             pltpu.VMEM(tiles.shape, F32),
@@ -391,7 +439,7 @@
             pltpu.VMEM((3, side, side), F32),
             pltpu.VMEM((q_all, 3 * side), BF16),
             pltpu.VMEM((side, 384), BF16),
-            pltpu.VMEM((q_all, side), F32),
+            pltpu.VMEM((8 * n_blk * fan, side), F32),
             pltpu.VMEM((384, side), F32),
             pltpu.VMEM((2, 9 * rows, side), F32),
             pltpu.VMEM((2, 9, rows, side), F32),
@@ -404,6 +452,19 @@
             pltpu.VMEM((n_col, n_row, 1, 8 * CAP), F32),
             pltpu.VMEM((n_col, n_row, 1, 8 * CAP), F32),
             pltpu.VMEM((n_dev, 8 * CAP), F32),
+            pltpu.VMEM((8 * n_blk, 4 * rows), BF16),
+            pltpu.VMEM((8 * n_blk, side), F32),
+            pltpu.VMEM((8 * n_blk * fan, side), F32),
+            pltpu.VMEM((8 * n_blk * fan, side), F32),
+            pltpu.VMEM((2, 8 * n_blk * fan, side), F32),
+            pltpu.VMEM((3, 8 * n_blk * fan, side), F32),
+            pltpu.SMEM((fan, n_blk), jnp.int32),
+            pltpu.VMEM(right_side.shape, F32),
+            pltpu.VMEM(anchor.shape, F32),
+            pltpu.VMEM(owners.shape, jnp.int32),
+            pltpu.VMEM(row_offset.shape, jnp.int32),
+            pltpu.VMEM(col_offset.shape, jnp.int32),
+            dma((6,)),
             dma((n_blk,)),
             dma((3, 9)), dma((3, 9)), dma((3, 9)), dma((3, 9)),
             dma((3, n_row)), dma((3, n_row)), dma((3, n_col)), dma((3, n_col)),
@@ -652,7 +713,7 @@
         copy.wait_send()
 
 
-CHUNK = 128
+CHUNK = 256
 BAND = 256
 
 
@@ -700,11 +761,9 @@
 
 
 def per_device(right_side, anchor, tiles, neighbours, owners, row_offset, col_offset, macro_density):
-    n_blk, _, side, _ = tiles.shape[0], tiles.shape[1], tiles.shape[2], tiles.shape[3]
     n_row, n_col = lax.axis_size("row"), lax.axis_size("col")
     solution, arrived = solve(
-        n_row, n_col, neighbours, right_side, anchor, owners.reshape(n_blk, side),
-        row_offset.reshape(n_blk, side), col_offset.reshape(n_blk, side), tiles,
+        n_row, n_col, neighbours.T, right_side, anchor, owners.T, row_offset, col_offset, tiles,
     )
     return solution, spread_and_diffuse(n_row, n_col, arrived, macro_density)
 

time: 106 us -> 95.4 us (0.900)
  Pallas kernels: 96.3 us -> 87.5 us
  other arithmetic: 1.36 us -> 0 us
    pallas_call x1, Pallas kernels: 62.8 us -> 55.7 us  [solve(): pl.pallas_call(functools.partial(solve_kernel, n_row, n_col), name='solve...]
    pallas_call x1, Pallas kernels: 33.5 us -> 31.8 us  [spread_and_diffuse(): pl.pallas_call(functools.partial(grid_kernel, n_row, n_col), name='spread...]
    unnamed x8 -> x14, local copies, waits for them, and re-layouts: 5.3 us -> 6.8 us
    reshape x3 -> x0, local copies, waits for them, and re-layouts: 1.41 us -> none  [the longest x1 0.7 us: per_device(): row_offset.reshape(n_blk, side)]
    unnamed x1 -> x0, other arithmetic: 1.36 us -> none
where the time goes in v4:
time: 95.4 us; the launch traced here: 95 us
  Pallas kernels  87.5 us (92%)
  local copies, waits for them, and re-layouts  6.8 us (7%)
    pallas_call x1, Pallas kernels, solve(): pl.pallas_call(functools.partial(solve_kernel, n_row, n_col), name='solve...  55.7 us
    pallas_call x1, Pallas kernels, spread_and_diffuse(): pl.pallas_call(functools.partial(grid_kernel, n_row, n_col), name='spread...  31.8 us
    unnamed x14, local copies, waits for them, and re-layouts  6.8 us

profile of v4, /device:TPU:1, one launch (start us, length us, event | category | flops | bytes accessed | tf_op | source)
XLA Modules:
  0.0 95.0 jit_solution(1099515164711015588)
XLA Ops:
  0.6 0.0 copy-start
  0.6 0.7 copy-done
  1.4 0.0 copy-start.1
  1.4 0.7 copy-done.1
  2.0 0.0 copy-start.2
  2.0 0.7 copy-done.2
  2.7 0.0 copy-start.3
  2.7 0.7 copy-done.3
  3.4 0.0 copy-start.4
  3.4 0.7 copy-done.4
  4.1 0.0 copy-start.5
  4.1 0.7 copy-done.5
  4.8 55.7 %solve_and_route.1 = (f32[8,2,256]{2,1,0:T(2,128)S(1)}, f32[128,128]{1,0:T(8,128)S(1)}) custom-call(s32[4,8]{1,0:T(4,128)S(1)} %bitcast.3, f32[8,2,256]{2,1,0:T(2,128)S(1)} %copy-done, f32[8,256]{1,0:T(8,128)S(1)} %copy-done.1, s32[1,2048]{1,0:T(1,128)S(1)} %bitcast.2, s32[2048]{0:T(1024)S(1)} %copy-done.3, s32[2048]{0:T(1024)S(1)} %copy-done.4, ...), custom_call_target="tpu_custom_call" | custom-call | flops 1000000000 | bytes 8388608 | tf_op jit(solution)/shard_map/solve_and_route/pallas_call | solution.py:426
  60.5 31.8 %spread_and_diffuse.1 = f32[2048,512]{1,0:T(8,128)S(1)} custom-call(f32[128,128]{1,0:T(8,128)S(1)} %get-tuple-element.5.pos_ref, f32[2048,512]{1,0:T(8,128)} %macro_ref.1), custom_call_target="tpu_custom_call" | custom-call | flops 10000000000 | bytes 8388608 | tf_op jit(solution)/shard_map/spread_and_diffuse/pallas_call | solution.py:725
  92.3 0.6 copy.12
  93.0 2.0 %copy.13 = f32[2048,512]{1,0:T(8,128)} copy(f32[2048,512]{1,0:T(8,128)S(1)} %spread_and_diffuse.1) | data formatting | bytes 8388608
Async XLA Ops:
  0.6 0.7 copy-start
  1.4 0.7 copy-start.1
  2.0 0.7 copy-start.2
  2.7 0.7 copy-start.3
  3.4 0.7 copy-start.4
  4.1 0.7 copy-start.5

commit v5 on v4

--- a/solution.py
+++ b/solution.py
@@ -106,43 +106,6 @@
         own_hot[b] = turned.astype(BF16)
         held = held + jnp.sum(turned, axis=0, keepdims=True)
 
-    pl.semaphore_wait(barrier, len(peers))
-
-    def x_rows(it, g):
-        return xbuf.at[it, pl.ds(g * rows, rows)]
-
-    pending = []
-
-    def forward(it):
-        for g in around:
-            dr, dc = AROUND[g]
-            copy = remote(
-                x_rows(it, 4), x_rows(it, 8 - g), fs.at[it, g], fr.at[it, 8 - g],
-                lax.rem(me_r + dr + n_row, n_row), lax.rem(me_c + dc + n_col, n_col),
-            )
-            copy.start()
-            pending.append(copy)
-
-    def forward_wait(it):
-        for g in around:
-            remote(x_rows(it, 4), x_rows(it, g), fs.at[it, g], fr.at[it, g], me_r, me_c).wait_recv()
-
-    def backward(it):
-        for g in around:
-            dr, dc = AROUND[g]
-            copy = remote(
-                back.at[it, pl.ds(g * rows, rows)], recv.at[it, 8 - g], bs.at[it, g], br.at[it, 8 - g],
-                lax.rem(me_r + dr + n_row, n_row), lax.rem(me_c + dc + n_col, n_col),
-            )
-            copy.start()
-            pending.append(copy)
-
-    def backward_wait(it):
-        for g in around:
-            remote(back.at[it, pl.ds(g * rows, rows)], recv.at[it, g], bs.at[it, g], br.at[it, g], me_r, me_c).wait_recv()
-
-    forward(0)
-
     ones_row = 9 * rows
     lane3 = iota((8, 3 * side), 1)
     part_row = iota((8, 1), 0)
@@ -172,6 +135,43 @@
     sel_t = sel[:, 0:side].astype(F32) + sel[:, side:2 * side].astype(F32) + sel[:, 2 * side:].astype(F32)
     spread_sel[...] = jnp.transpose(jnp.concatenate([sel_t, jnp.zeros((384 - q_all, side), F32)], axis=0)).astype(BF16)
     terms[...] = jnp.zeros_like(terms)
+
+    pl.semaphore_wait(barrier, len(peers))
+
+    def x_rows(it, g):
+        return xbuf.at[it, pl.ds(g * rows, rows)]
+
+    pending = []
+
+    def forward(it):
+        for g in around:
+            dr, dc = AROUND[g]
+            copy = remote(
+                x_rows(it, 4), x_rows(it, 8 - g), fs.at[it, g], fr.at[it, 8 - g],
+                lax.rem(me_r + dr + n_row, n_row), lax.rem(me_c + dc + n_col, n_col),
+            )
+            copy.start()
+            pending.append(copy)
+
+    def forward_wait(it):
+        for g in around:
+            remote(x_rows(it, 4), x_rows(it, g), fs.at[it, g], fr.at[it, g], me_r, me_c).wait_recv()
+
+    def backward(it):
+        for g in around:
+            dr, dc = AROUND[g]
+            copy = remote(
+                back.at[it, pl.ds(g * rows, rows)], recv.at[it, 8 - g], bs.at[it, g], br.at[it, 8 - g],
+                lax.rem(me_r + dr + n_row, n_row), lax.rem(me_c + dc + n_col, n_col),
+            )
+            copy.start()
+            pending.append(copy)
+
+    def backward_wait(it):
+        for g in around:
+            remote(back.at[it, pl.ds(g * rows, rows)], recv.at[it, g], bs.at[it, g], br.at[it, g], me_r, me_c).wait_recv()
+
+    forward(0)
 
     def split_block(b, carry):
         pltpu.make_async_copy(tiles_ref.at[b], stage.at[b], tile_sem.at[b]).wait()
@@ -471,7 +471,7 @@
             dma((n_row,)), dma((n_row,)), dma((n_col,)), dma((n_col,)), dma((2,)),
         ],
         compiler_params=pltpu.CompilerParams(
-            collective_id=0, has_side_effects=True, vmem_limit_bytes=48 * 2**20
+            collective_id=0, has_side_effects=True, vmem_limit_bytes=63480000
         ),
         cost_estimate=pl.CostEstimate(flops=10**9, bytes_accessed=2**23, transcendentals=0),
     )(neighbours, right_side, anchor, owners, row_offset, col_offset, tiles)
@@ -479,10 +479,10 @@
 
 def grid_kernel(
     n_row, n_col,
-    pos_ref, macro_ref, out_ref,
-    one, two, bell_col, left_sel, right_sel, low_part, high_part, place,
-    top_s, bottom_s, west_s, east_s, up_r, down_r, west_r, east_r, keep_top, keep_bottom, side,
-    in_sem, out_sem, ss, rs,
+    pos_ref, macro_ref, two, side, rims,
+    one, bell_col, left_sel, right_sel, low_part, high_part, place,
+    top_s, bottom_s, west_s, east_s, up_r, down_r, west_r, east_r, keep_top, keep_bottom,
+    in_sem, ss, rs,
 ):
     length, width = macro_ref.shape
     n_dev = n_row * n_col
@@ -498,11 +498,6 @@
     def load(i):
         return pltpu.make_async_copy(
             macro_ref.at[pl.ds(i * BAND, BAND)], one.at[pl.ds(8 + i * BAND, BAND)], in_sem.at[i]
-        )
-
-    def store(buf, i):
-        return pltpu.make_async_copy(
-            buf.at[pl.ds(8 + i * CHUNK, CHUNK)], out_ref.at[pl.ds(i * CHUNK, CHUNK)], out_sem.at[i]
         )
 
     barrier = pltpu.get_barrier_semaphore()
@@ -609,13 +604,6 @@
         copy.start()
         copies.append(copy)
 
-    def summed(src, begin, n):
-        window = src[pl.ds(pl.multiple_of(begin - 8, 8), n + 16), :]
-        centre = window[8:8 + n]
-        return (
-            (centre + window[7:7 + n]) + (window[9:9 + n] + pltpu.roll(centre, 1, 1)) + pltpu.roll(centre, width - 1, 1)
-        )
-
     for src, dst in ((one, two), (two, one), (one, two)):
 
         def strip(i, carry, src=src, dst=dst):
@@ -668,49 +656,85 @@
                 r = r * flag
         return (r[8:16] if at_top else r[8:16]) * scale
 
+    rims[0:8, :] = rim_rows(up_r[...], keep_top[...], not_first_row, True)
+    rims[8:16, :] = rim_rows(down_r[...], keep_bottom[...], not_last_row, False)
+    for copy in copies:
+        copy.wait_send()
+
+
+def summed(src, begin, n):
+    width = src.shape[1]
+    window = src[pl.ds(pl.multiple_of(begin - 8, 8), n + 16), :]
+    centre = window[8:8 + n]
+    return (
+        (centre + window[7:7 + n]) + (window[9:9 + n] + pltpu.roll(centre, 1, 1)) + pltpu.roll(centre, width - 1, 1)
+    )
+
+
+def last_step_kernel(two, side, rims, out_ref, one, out_sem):
+    length, width = out_ref.shape
+    n_chunk = length // CHUNK
+    scale = 0.2 ** STEPS
+    lane = iota((1, 128), 1)
+
+    def store(i):
+        here = pl.ds(pl.multiple_of(i * CHUNK, CHUNK), CHUNK)
+        return pltpu.make_async_copy(one.at[here], out_ref.at[here], out_sem.at[i])
+
     zero112 = jnp.zeros((112, 128), F32)
 
-    def side_tile(i):
-        here = pl.ds(pl.multiple_of((i + 1) * 128, 128), 128)
-        return jnp.transpose(jnp.concatenate([side[8:16, here], zero112, side[16:24, here]], axis=0))
-
     def finish(i, carry):
-        begin = pl.multiple_of(8 + i * CHUNK, 8)
-        total = summed(two, begin, CHUNK) * scale
+        total = summed(two, pl.multiple_of(8 + i * CHUNK, 8), CHUNK) * scale
         for h in range(CHUNK // 128):
             rows_h = slice(h * 128, (h + 1) * 128)
-            tile = side_tile(i * (CHUNK // 128) + h)
-            here = pl.ds(pl.multiple_of(begin + h * 128, 8), 128)
+            at_lane = pl.ds(pl.multiple_of(i * CHUNK + (h + 1) * 128, 128), 128)
+            tile = jnp.transpose(jnp.concatenate([side[8:16, at_lane], zero112, side[16:24, at_lane]], axis=0))
+            here = pl.ds(pl.multiple_of(i * CHUNK + h * 128, 8), 128)
             one[here, 0:128] = jnp.where(lane < 4, tile, total[rows_h, 0:128])
             one[here, 128:width - 128] = total[rows_h, 128:width - 128]
             one[here, width - 128:width] = jnp.where(lane >= 124, tile, total[rows_h, width - 128:width])
         return carry
 
+    def rim(at_row, rim8):
+        here = slice(at_row, at_row + 8)
+        one[here, 0:128] = jnp.where(lane < 4, one[here, 0:128], rim8[:, 0:128])
+        one[here, 128:width - 128] = rim8[:, 128:width - 128]
+        one[here, width - 128:width] = jnp.where(lane >= 124, one[here, width - 128:width], rim8[:, width - 128:width])
+
+    finish(jnp.int32(0), 0)
+    rim(0, rims[0:8, :])
+    store(0).start()
+
     def start_store(i, carry):
         finish(i, carry)
-        store(one, i).start()
+        store(i).start()
         return carry
 
     lax.fori_loop(1, n_chunk - 1, start_store, 0)
-    for i, at_row8, rim8 in (
-        (0, 8, rim_rows(up_r[...], keep_top[...], not_first_row, True)),
-        (n_chunk - 1, length, rim_rows(down_r[...], keep_bottom[...], not_last_row, False)),
-    ):
-        finish(jnp.int32(i), 0)
-        one[at_row8:at_row8 + 8, 0:128] = jnp.where(lane < 4, one[at_row8:at_row8 + 8, 0:128], rim8[:, 0:128])
-        one[at_row8:at_row8 + 8, 128:width - 128] = rim8[:, 128:width - 128]
-        one[at_row8:at_row8 + 8, width - 128:width] = jnp.where(
-            lane >= 124, one[at_row8:at_row8 + 8, width - 128:width], rim8[:, width - 128:width]
-        )
-        store(one, i).start()
+    finish(jnp.int32(n_chunk - 1), 0)
+    rim(length - 8, rims[8:16, :])
+    store(n_chunk - 1).start()
 
     def finish_store(i, carry):
-        store(one, i).wait()
+        store(i).wait()
         return carry
 
     lax.fori_loop(0, n_chunk, finish_store, 0)
-    for copy in copies:
-        copy.wait_send()
+
+
+def last_step(three, side, rims):
+    length, width = three.shape[0] - 16, three.shape[1]
+    vmem = pl.BlockSpec(memory_space=pltpu.VMEM)
+    return pl.pallas_call(
+        last_step_kernel,
+        name="last_step",
+        out_shape=jax.ShapeDtypeStruct((length, width), F32),
+        in_specs=[vmem] * 3,
+        out_specs=pl.BlockSpec(memory_space=pl.ANY),
+        scratch_shapes=[pltpu.VMEM((length, width), F32), pltpu.SemaphoreType.DMA((length // CHUNK,))],
+        compiler_params=pltpu.CompilerParams(vmem_limit_bytes=16 * 2**20),
+        cost_estimate=pl.CostEstimate(flops=5 * length * width, bytes_accessed=8 * length * width, transcendentals=0),
+    )(three, side, rims)
 
 
 CHUNK = 256
@@ -721,15 +745,19 @@
     length, width = macro.shape
     n_slot = n_row * n_col * CAP
     any_space = pl.BlockSpec(memory_space=pl.ANY)
+    vmem = pl.BlockSpec(memory_space=pltpu.VMEM)
     dma = pltpu.SemaphoreType.DMA
     return pl.pallas_call(
         functools.partial(grid_kernel, n_row, n_col),
         name="spread_and_diffuse",
-        out_shape=jax.ShapeDtypeStruct(macro.shape, F32),
-        in_specs=[pl.BlockSpec(memory_space=pltpu.VMEM), any_space],
-        out_specs=any_space,
+        out_shape=(
+            jax.ShapeDtypeStruct((length + 16, width), F32),
+            jax.ShapeDtypeStruct((32, length + 256), F32),
+            jax.ShapeDtypeStruct((16, width), F32),
+        ),
+        in_specs=[vmem, any_space],
+        out_specs=(vmem,) * 3,
         scratch_shapes=[
-            pltpu.VMEM((length + 16, width), F32),
             pltpu.VMEM((length + 16, width), F32),
             pltpu.VMEM((n_slot, width), BF16),
             pltpu.VMEM((BAND, n_slot), BF16),
@@ -747,14 +775,12 @@
             pltpu.VMEM((8, length + 256), F32),
             pltpu.VMEM((16, width), F32),
             pltpu.VMEM((16, width), F32),
-            pltpu.VMEM((32, length + 256), F32),
             dma((length // BAND,)),
-            dma((length // CHUNK,)),
             dma((9,)),
             dma((9,)),
         ],
         compiler_params=pltpu.CompilerParams(
-            collective_id=1, has_side_effects=True, vmem_limit_bytes=48 * 2**20
+            collective_id=1, has_side_effects=True, vmem_limit_bytes=24 * 2**20
         ),
         cost_estimate=pl.CostEstimate(flops=10**10, bytes_accessed=8 * length * width, transcendentals=0),
     )(positions, macro)
@@ -765,7 +791,7 @@
     solution, arrived = solve(
         n_row, n_col, neighbours.T, right_side, anchor, owners.T, row_offset, col_offset, tiles,
     )
-    return solution, spread_and_diffuse(n_row, n_col, arrived, macro_density)
+    return solution, last_step(*spread_and_diffuse(n_row, n_col, arrived, macro_density))
 
 
 def solution(mesh):

time: 95.4 us -> 93.2 us (0.977)
  local copies, waits for them, and re-layouts: 6.8 us -> 3.63 us
  Pallas kernels: 87.5 us -> 88.7 us
    pallas_call x0 -> x1, Pallas kernels: none -> 4.36 us  [last_step(): pl.pallas_call(last_step_kernel, name='last_step', out_shape=jax.ShapeDty...]
    pallas_call x1, Pallas kernels: 31.8 us -> 28 us  [spread_and_diffuse(): pl.pallas_call(functools.partial(grid_kernel, n_row, n_col), name='spread...]
    unnamed x14 -> x7, local copies, waits for them, and re-layouts: 6.8 us -> 3.63 us
where the time goes in v5:
time: 93.2 us; the launch traced here: 93.1 us
  Pallas kernels  88.7 us (95%)
  local copies, waits for them, and re-layouts  3.63 us (4%)
    pallas_call x1, Pallas kernels, solve(): pl.pallas_call(functools.partial(solve_kernel, n_row, n_col), name='solve...  56.4 us
    pallas_call x1, Pallas kernels, spread_and_diffuse(): pl.pallas_call(functools.partial(grid_kernel, n_row, n_col), name='spread...  28 us
    pallas_call x1, Pallas kernels, last_step(): pl.pallas_call(last_step_kernel, name='last_step', out_shape=jax.ShapeDty...  4.36 us
    unnamed x7, local copies, waits for them, and re-layouts  3.63 us

profile of v5, /device:TPU:1, one launch (start us, length us, event | category | flops | bytes accessed | tf_op | source)
XLA Modules:
  0.0 93.1 jit_solution(14404345265385305358)
XLA Ops:
  0.6 56.4 %solve_and_route.1 = (f32[8,2,256]{2,1,0:T(2,128)}, f32[128,128]{1,0:T(8,128)}) custom-call(s32[4,8]{1,0:T(4,128)} %bitcast.3, f32[8,2,256]{2,1,0:T(2,128)} %rhs_hbm.1, f32[8,256]{1,0:T(8,128)} %anchor_hbm.1, s32[1,2048]{1,0:T(1,128)} %bitcast.2, s32[2048]{0:T(1024)} %roff_hbm.1, s32[2048]{0:T(1024)} %coff_hbm.1, f32[8,4,256,256]{3,2,1,0:T(8,128)} %tiles_ref.1), custom_call_target="tpu_custom_call" | custom-call | flops 1000000000 | bytes 8388608 | tf_op jit(solution)/shard_map/solve_and_route/pallas_call | solution.py:426
  57.0 0.0 copy-start
  57.1 2.2 %copy-done = f32[2048,512]{1,0:T(8,128)S(1)} copy-done((f32[2048,512]{1,0:T(8,128)S(1)}, f32[2048,512]{1,0:T(8,128)}, u32[]{:S(2)}) %copy-start) | copy-done | bytes 4194328
  59.2 0.0 copy-start.1
  59.2 0.8 copy-done.1
  60.1 28.0 %spread_and_diffuse.1 = (f32[2064,512]{1,0:T(8,128)S(1)}, f32[32,2304]{1,0:T(8,128)S(1)}, f32[16,512]{1,0:T(8,128)S(1)}) custom-call(f32[128,128]{1,0:T(8,128)S(1)} %copy-done.1, f32[2048,512]{1,0:T(8,128)S(1)} %copy-done), custom_call_target="tpu_custom_call" | custom-call | flops 10000000000 | bytes 8388608 | tf_op jit(solution)/shard_map/spread_and_diffuse/pallas_call | solution.py:750
  88.1 0.0 copy-start.2
  88.1 4.4 %last_step.1 = f32[2048,512]{1,0:T(8,128)} custom-call(f32[2064,512]{1,0:T(8,128)S(1)} %get-tuple-element.9.two, f32[32,2304]{1,0:T(8,128)S(1)} %get-tuple-element.10.side, f32[16,512]{1,0:T(8,128)S(1)} %get-tuple-element.11.rims), custom_call_target="tpu_custom_call" | custom-call | flops 5242880 | bytes 8388608 | tf_op jit(solution)/shard_map/last_step/pallas_call | solution.py:728
  92.4 0.0 copy-done.2
  92.4 0.6 copy.11
Async XLA Ops:
  57.0 2.2 %copy-start = (f32[2048,512]{1,0:T(8,128)S(1)}, f32[2048,512]{1,0:T(8,128)}, u32[]{:S(2)}) copy-start(f32[2048,512]{1,0:T(8,128)} %macro_ref.1) | copy-start | bytes 12582916
  59.2 0.8 copy-start.1
  88.1 4.4 %copy-start.2 = (f32[8,2,256]{2,1,0:T(2,128)S(1)}, f32[8,2,256]{2,1,0:T(2,128)}, u32[]{:S(2)}) copy-start(f32[8,2,256]{2,1,0:T(2,128)} %get-tuple-element.14) | copy-start | bytes 49156

commit v6 on v5

--- a/solution.py
+++ b/solution.py
@@ -182,7 +182,7 @@
             tlo[b, k] = (t - hi.astype(F32)).astype(BF16)
         return carry
 
-    lax.fori_loop(0, n_blk, split_block, 0)
+    lax.fori_loop(0, n_blk, split_block, 0, unroll=2)
 
     first_row = jnp.where(iota((rows, side), 0) == 0, 1.0, 0.0).astype(BF16)
 
@@ -205,7 +205,7 @@
                     sums_sc[pl.ds(q, 8), :] = jnp.broadcast_to(down[6:7, :], (8, side))
             return carry
 
-        lax.fori_loop(0, n_blk, one_block, 0, unroll=2)
+        lax.fori_loop(0, n_blk, one_block, 0, unroll=8)
         down_sum[it] = over_parts(down_sc[...])
 
     def gather_far(it):
@@ -231,7 +231,7 @@
             terms[pl.ds(pl.multiple_of(q_own + b * 8, 8), 8), :] = weight * own - total
             return carry
 
-        lax.fori_loop(0, n_blk, one_block, 0, unroll=2)
+        lax.fori_loop(0, n_blk, one_block, 0, unroll=4)
         terms[0:q_own, :] = sums_sc[...] * gath[...] - down_sc[...]
         hi, mid, low = split3(terms[...])
         where_to = spread_sel[0:9 * rows, :]
@@ -534,14 +534,14 @@
 
     def some_columns(i, carry):
         p, m = carry
-        for k in range(4):
+        for k in range(8):
             d = v - p[:, k:k + 1]
             inside = jnp.abs(v - m[:, k:k + 1]) < 8.0
             bell = jnp.where(inside, jnp.exp2(d * d * (-0.5 * log2e)), 0.0)
-            bell_col[pl.ds(pl.multiple_of((i * 4 + k) * n_dev, n_dev), n_dev), :] = bell.astype(BF16)
-        return pltpu.roll(p, 124, 1), pltpu.roll(m, 124, 1)
-
-    lax.fori_loop(0, CAP // 4, some_columns, (at_col, middle))
+            bell_col[pl.ds(pl.multiple_of((i * 8 + k) * n_dev, n_dev), n_dev), :] = bell.astype(BF16)
+        return pltpu.roll(p, 120, 1), pltpu.roll(m, 120, 1)
+
+    lax.fori_loop(0, CAP // 8, some_columns, (at_col, middle))
 
     def build(dst, band):
         for sub in range(BAND // 32):
@@ -607,11 +607,11 @@
     for src, dst in ((one, two), (two, one), (one, two)):
 
         def strip(i, carry, src=src, dst=dst):
-            begin = pl.multiple_of(8 + i * CHUNK, 8)
-            dst[pl.ds(begin, CHUNK), :] = summed(src, begin, CHUNK)
+            begin = pl.multiple_of(8 + i * STRIP, 8)
+            dst[pl.ds(begin, STRIP), :] = summed(src, begin, STRIP)
             return carry
 
-        lax.fori_loop(0, n_chunk, strip, 0)
+        lax.fori_loop(0, length // STRIP, strip, 0)
 
     for copy in copies:
         copy.wait_recv()
@@ -738,6 +738,7 @@
 
 
 CHUNK = 256
+STRIP = 512
 BAND = 256
 
 

time: 93.2 us -> 92.1 us (0.988)
  Pallas kernels: 88.7 us -> 87.6 us
where the time goes in v6:
time: 92.1 us; the launch traced here: 91.9 us
  Pallas kernels  87.6 us (95%)
  local copies, waits for them, and re-layouts  3.63 us (4%)
    pallas_call x1, Pallas kernels, solve(): pl.pallas_call(functools.partial(solve_kernel, n_row, n_col), name='solve...  55.9 us
    pallas_call x1, Pallas kernels, spread_and_diffuse(): pl.pallas_call(functools.partial(grid_kernel, n_row, n_col), name='spread...  27.3 us
    pallas_call x1, Pallas kernels, last_step(): pl.pallas_call(last_step_kernel, name='last_step', out_shape=jax.ShapeDty...  4.36 us
    unnamed x7, local copies, waits for them, and re-layouts  3.63 us

profile of v6, /device:TPU:1, one launch (start us, length us, event | category | flops | bytes accessed | tf_op | source)
XLA Modules:
  0.0 91.9 jit_solution(13283403652833206348)
XLA Ops:
  0.6 55.9 %solve_and_route.1 = (f32[8,2,256]{2,1,0:T(2,128)}, f32[128,128]{1,0:T(8,128)}) custom-call(s32[4,8]{1,0:T(4,128)} %bitcast.3, f32[8,2,256]{2,1,0:T(2,128)} %rhs_hbm.1, f32[8,256]{1,0:T(8,128)} %anchor_hbm.1, s32[1,2048]{1,0:T(1,128)} %bitcast.2, s32[2048]{0:T(1024)} %roff_hbm.1, s32[2048]{0:T(1024)} %coff_hbm.1, f32[8,4,256,256]{3,2,1,0:T(8,128)} %tiles_ref.1), custom_call_target="tpu_custom_call" | custom-call | flops 1000000000 | bytes 8388608 | tf_op jit(solution)/shard_map/solve_and_route/pallas_call | solution.py:426
  56.6 0.0 copy-start
  56.6 2.2 %copy-done = f32[2048,512]{1,0:T(8,128)S(1)} copy-done((f32[2048,512]{1,0:T(8,128)S(1)}, f32[2048,512]{1,0:T(8,128)}, u32[]{:S(2)}) %copy-start) | copy-done | bytes 4194328
  58.8 0.0 copy-start.1
  58.8 0.8 copy-done.1
  59.6 27.3 %spread_and_diffuse.1 = (f32[2064,512]{1,0:T(8,128)S(1)}, f32[32,2304]{1,0:T(8,128)S(1)}, f32[16,512]{1,0:T(8,128)S(1)}) custom-call(f32[128,128]{1,0:T(8,128)S(1)} %copy-done.1, f32[2048,512]{1,0:T(8,128)S(1)} %copy-done), custom_call_target="tpu_custom_call" | custom-call | flops 10000000000 | bytes 8388608 | tf_op jit(solution)/shard_map/spread_and_diffuse/pallas_call | solution.py:751
  86.9 0.0 copy-start.2
  86.9 4.4 %last_step.1 = f32[2048,512]{1,0:T(8,128)} custom-call(f32[2064,512]{1,0:T(8,128)S(1)} %get-tuple-element.9.two, f32[32,2304]{1,0:T(8,128)S(1)} %get-tuple-element.10.side, f32[16,512]{1,0:T(8,128)S(1)} %get-tuple-element.11.rims), custom_call_target="tpu_custom_call" | custom-call | flops 5242880 | bytes 8388608 | tf_op jit(solution)/shard_map/last_step/pallas_call | solution.py:728
  91.3 0.0 copy-done.2
  91.3 0.6 copy.11
Async XLA Ops:
  56.6 2.2 %copy-start = (f32[2048,512]{1,0:T(8,128)S(1)}, f32[2048,512]{1,0:T(8,128)}, u32[]{:S(2)}) copy-start(f32[2048,512]{1,0:T(8,128)} %macro_ref.1) | copy-start | bytes 12582916
  58.8 0.8 copy-start.1
  86.9 4.4 %copy-start.2 = (f32[8,2,256]{2,1,0:T(2,128)S(1)}, f32[8,2,256]{2,1,0:T(2,128)}, u32[]{:S(2)}) copy-start(f32[8,2,256]{2,1,0:T(2,128)} %get-tuple-element.14) | copy-start | bytes 49156

commit v7 on v6

--- a/solution.py
+++ b/solution.py
@@ -319,7 +319,11 @@
     dots_start(0, [(r0, r0), (r0, w0)])
     own_products(1, w0)
     apply(1, lambda: dots_middle(0))
-    table_w0 = by_owner(both(w0))
+    early = jnp.transpose(jnp.concatenate([table_r0, by_owner(both(w0))], axis=0))
+    for o in range(n_dev):
+        out_rows[o // n_col, o % n_col, :, 0:4 * CAP] = early[o:o + 1, :]
+    empty = iota((CAP, n_dev), 0).astype(F32) >= held
+    table_off = jnp.concatenate([jnp.where(empty, NONE, table_off[0:CAP]), table_off[CAP:]], axis=0)
     gamma0, curve0 = dots_end(0, 2)
     alpha0 = gamma0 / curve0
     z0 = applied(1)
@@ -329,14 +333,9 @@
     dots_start(1, [(r1, r1), (r1, w1), (r1, w0)])
     forward(2)
 
-    table = jnp.concatenate([table_r0, table_w0, by_owner(both(w1)), table_off], axis=0)
-    empty = iota((CAP, n_dev), 0).astype(F32) >= held
-    table = jnp.concatenate(
-        [table[0:6 * CAP], jnp.where(empty, NONE, table[6 * CAP:7 * CAP]), table[7 * CAP:]], axis=0
-    )
-    table = jnp.transpose(table)
+    late = jnp.transpose(jnp.concatenate([by_owner(both(w1)), table_off], axis=0))
     for o in range(n_dev):
-        out_rows[o // n_col, o % n_col] = table[o:o + 1, :]
+        out_rows[o // n_col, o % n_col, :, 4 * CAP:8 * CAP] = late[o:o + 1, :]
     keep = pltpu.make_async_copy(out_rows.at[me_r], mid_rows.at[:, me_r], keep_sem.at[0])
     keep.start()
     for d in row_order:
@@ -365,6 +364,8 @@
     far_r1 = far_sum[0] - grouped(alpha0, far_sum[1])
     down_r1 = down_sum[0] - grouped(alpha0, down_sum[1])
     far_w1 = over_parts(gath[...])
+    weights = weight_sc[...]
+    weights = jnp.concatenate([weights[b:b + 1] for b in range(n_blk) for _ in (0, 1)], axis=0)
     gamma1, r1w1, r1w0 = dots_end(1, 3)
     beta0 = gamma1 / gamma0
     curve1 = r1w1 + 2.0 * beta0 * r1w0 + beta0 * beta0 * curve0
@@ -378,8 +379,6 @@
     cross = far_r2 * (sums_sc[...] * far_r2 - 2.0 * down_r2)
     cross = jnp.sum(cross.reshape(q_own // 8, 8, side), axis=0)
     cross = jnp.where(iota((8, side), 0) < 2, cross, 0.0)
-    weights = weight_sc[...]
-    weights = jnp.concatenate([weights[b:b + 1] for b in range(n_blk) for _ in (0, 1)], axis=0)
     dots_start(2, [(r2, weights * r2), (r2, r2), (r2, s1)], more=cross)
 
     keep2.wait()

time: 92.1 us -> 92.1 us (level)
  no operation moved by 1% of the time
where the time goes in v7:
time: 92.1 us; the launch traced here: 91.9 us
  Pallas kernels  87.6 us (95%)
  local copies, waits for them, and re-layouts  3.63 us (4%)
    pallas_call x1, Pallas kernels, solve(): pl.pallas_call(functools.partial(solve_kernel, n_row, n_col), name='solve...  55.9 us
    pallas_call x1, Pallas kernels, spread_and_diffuse(): pl.pallas_call(functools.partial(grid_kernel, n_row, n_col), name='spread...  27.3 us
    pallas_call x1, Pallas kernels, last_step(): pl.pallas_call(last_step_kernel, name='last_step', out_shape=jax.ShapeDty...  4.36 us
    unnamed x7, local copies, waits for them, and re-layouts  3.63 us

profile of v7, /device:TPU:1, one launch (start us, length us, event | category | flops | bytes accessed | tf_op | source)
XLA Modules:
  0.0 91.9 jit_solution(9888494853439670497)
XLA Ops:
  0.6 55.9 %solve_and_route.1 = (f32[8,2,256]{2,1,0:T(2,128)}, f32[128,128]{1,0:T(8,128)}) custom-call(s32[4,8]{1,0:T(4,128)} %bitcast.3, f32[8,2,256]{2,1,0:T(2,128)} %rhs_hbm.1, f32[8,256]{1,0:T(8,128)} %anchor_hbm.1, s32[1,2048]{1,0:T(1,128)} %bitcast.2, s32[2048]{0:T(1024)} %roff_hbm.1, s32[2048]{0:T(1024)} %coff_hbm.1, f32[8,4,256,256]{3,2,1,0:T(8,128)} %tiles_ref.1), custom_call_target="tpu_custom_call" | custom-call | flops 1000000000 | bytes 8388608 | tf_op jit(solution)/shard_map/solve_and_route/pallas_call | solution.py:425
  56.5 0.0 copy-start
  56.6 2.2 %copy-done = f32[2048,512]{1,0:T(8,128)S(1)} copy-done((f32[2048,512]{1,0:T(8,128)S(1)}, f32[2048,512]{1,0:T(8,128)}, u32[]{:S(2)}) %copy-start) | copy-done | bytes 4194328
  58.7 0.0 copy-start.1
  58.7 0.8 copy-done.1
  59.6 27.3 %spread_and_diffuse.1 = (f32[2064,512]{1,0:T(8,128)S(1)}, f32[32,2304]{1,0:T(8,128)S(1)}, f32[16,512]{1,0:T(8,128)S(1)}) custom-call(f32[128,128]{1,0:T(8,128)S(1)} %copy-done.1, f32[2048,512]{1,0:T(8,128)S(1)} %copy-done), custom_call_target="tpu_custom_call" | custom-call | flops 10000000000 | bytes 8388608 | tf_op jit(solution)/shard_map/spread_and_diffuse/pallas_call | solution.py:750
  86.9 0.0 copy-start.2
  86.9 4.4 %last_step.1 = f32[2048,512]{1,0:T(8,128)} custom-call(f32[2064,512]{1,0:T(8,128)S(1)} %get-tuple-element.9.two, f32[32,2304]{1,0:T(8,128)S(1)} %get-tuple-element.10.side, f32[16,512]{1,0:T(8,128)S(1)} %get-tuple-element.11.rims), custom_call_target="tpu_custom_call" | custom-call | flops 5242880 | bytes 8388608 | tf_op jit(solution)/shard_map/last_step/pallas_call | solution.py:727
  91.3 0.0 copy-done.2
  91.3 0.6 copy.11
Async XLA Ops:
  56.5 2.2 %copy-start = (f32[2048,512]{1,0:T(8,128)S(1)}, f32[2048,512]{1,0:T(8,128)}, u32[]{:S(2)}) copy-start(f32[2048,512]{1,0:T(8,128)} %macro_ref.1) | copy-start | bytes 12582916
  58.7 0.8 copy-start.1
  86.9 4.4 %copy-start.2 = (f32[8,2,256]{2,1,0:T(2,128)S(1)}, f32[8,2,256]{2,1,0:T(2,128)}, u32[]{:S(2)}) copy-start(f32[8,2,256]{2,1,0:T(2,128)} %get-tuple-element.14) | copy-start | bytes 49156
